TPU v7x, 128 devices: a whole 4x4x4 slice. The times are simulated.
128 devices in a mesh: dp: 4 (over z_lo, core), ctx: 32 (over x, y, z_hi).
Axes of the slice: x: 4, y: 4, z: 4 (z_hi: 2, z_lo: 2; z = z_hi * 2 + z_lo), core: 2. Of those that a mesh axis runs over, the one named last changes fastest.
Arguments:
- hidden_x: bfloat16 [4, 16384, 2048], P('dp', 'ctx'), may hold values from -6 to 6
- b_proj: bfloat16 [4, 16384, 256], P('dp', 'ctx'), may hold values from -0.5 to 0.5
- c_proj: bfloat16 [4, 16384, 256], P('dp', 'ctx'), may hold values from -0.5 to 0.5
- dt_raw: float32 [4, 16384, 64], P('dp', 'ctx'), may hold values from -3 to 3
- span_start: int32 [4, 16384], P('dp', 'ctx'), may hold values 0 or 1
- a_log: float32 [64], replicated, may hold values from -9 to -3.4
- skip_gain: float32 [64], replicated, may hold values from 0.5 to 1.5
- dt_bias: float32 [64], replicated, may hold values from -0.5 to 0.5
- out_grad: bfloat16 [4, 16384, 2048], P('dp', 'ctx'), may hold values from -6 to 6
Outputs:
- mixed: bfloat16 [4, 16384, 2048], P('dp', 'ctx')
- grad_x: bfloat16 [4, 16384, 2048], P('dp', 'ctx')
- grad_b: bfloat16 [4, 16384, 256], P('dp', 'ctx')
- grad_c: bfloat16 [4, 16384, 256], P('dp', 'ctx')
- grad_dt: float32 [4, 16384, 64], P('dp', 'ctx')
- grad_a_log: float32 [64], replicated
- grad_skip: float32 [64], replicated
- grad_dt_bias: float32 [64], replicated
All inputs are finite; a program needn't handle non-finite values. No bound on the sum of `span_start` on one device may be relied on, other than what follows from the above.
Results may differ from a plain program's by a relative error of at most 0.0095.
Values sent between devices are 32-bit elements; how exact they have to be, the bound alone decides.
A program may use at most 320 MiB of HBM per device.

v0:
```python
import jax
import jax.numpy as jnp
from jax import lax
from jax.sharding import PartitionSpec as P

H = 64
P_SIZE = 32
N = 64
G = 4
STRETCH = 256


def prefix(array, axis, combine, identity, reverse):
    peers, place = (lax.axis_size(axis), lax.axis_index(axis))
    everything = jax.tree.map(lambda part: lax.all_gather(part, axis), array)
    start = jax.tree.map(
        lambda part, zero: jnp.broadcast_to(jnp.asarray(zero, part.dtype), part.shape),
        array,
        identity,
    )

    def lap(k, before):
        at = peers - 1 - k if reverse else k
        reached = at > place if reverse else at < place
        new = combine(before, jax.tree.map(lambda part: part[at], everything))
        return jax.tree.map(lambda a, b: jnp.where(reached, a, b), new, before)

    return lax.fori_loop(0, peers, lap, start)


def decay_terms(dt_raw, starts, a_log, dt_bias):
    dt_step = jax.nn.softplus(dt_raw + dt_bias[None, :])
    decay_rate = -jnp.exp(a_log)
    cum_decay = jnp.cumsum(dt_step * decay_rate[None, :], axis=0)
    span_count = jnp.cumsum(starts, axis=0)
    return (dt_step, cum_decay, span_count)


def stretch_summary(x_rows, b_rows, dt_raw, starts, a_log, dt_bias):
    dt_step, cum_decay, span_count = decay_terms(dt_raw, starts, a_log, dt_bias)
    length = x_rows.shape[0]
    heads_per = H // G
    kept_rows = jnp.where(span_count == span_count[length - 1], 1.0, 0.0)
    weight = jnp.exp(cum_decay[length - 1][None, :] - cum_decay) * dt_step * kept_rows[:, None]
    carried = jnp.where(
        span_count[length - 1] == 0, jnp.exp(cum_decay[length - 1]), 0.0 * cum_decay[length - 1]
    )
    scaled = (
        x_rows.reshape(length, G, heads_per, P_SIZE)
        * weight.reshape(length, G, heads_per)[..., None]
    )
    state_sum = jnp.einsum(
        "tgkp,tgn->gkpn", scaled, b_rows.reshape(length, G, N), precision=lax.Precision.HIGHEST
    )
    return (carried, state_sum.reshape(H, P_SIZE, N))


def state_reach(c_rows, cum_decay, span_count):
    length = c_rows.shape[0]
    heads_per = H // G
    enters = jnp.where(span_count == 0, 1.0, 0.0)
    carry_reach = jnp.exp(cum_decay) * enters[:, None]
    return c_rows.reshape(length, G, 1, N) * carry_reach.reshape(length, G, heads_per, 1)


def stretch_output(x_rows, b_rows, c_rows, dt_raw, starts, state_in, a_log, skip_gain, dt_bias):
    dt_step, cum_decay, span_count = decay_terms(dt_raw, starts, a_log, dt_bias)
    length = x_rows.shape[0]
    heads_per = H // G
    x_half = x_rows.astype(jnp.bfloat16)
    b_half = b_rows.astype(jnp.bfloat16)
    c_half = c_rows.astype(jnp.bfloat16)
    scores = jnp.einsum(
        "tgn,sgn->gts",
        c_half.reshape(length, G, N),
        b_half.reshape(length, G, N),
        preferred_element_type=jnp.float32,
    )
    position = jnp.arange(length)
    visible = (position[:, None] >= position[None, :]) & (
        span_count[:, None] == span_count[None, :]
    )
    seen = visible[None, None]
    cum_heads = jnp.transpose(cum_decay).reshape(G, heads_per, length)
    dt_heads = jnp.transpose(dt_step).reshape(G, heads_per, length)
    log_gap = cum_heads[:, :, :, None] - cum_heads[:, :, None, :]
    log_gap = jnp.where(seen, log_gap, 0.0)
    factor = jnp.exp(log_gap) * jnp.where(seen, 1.0, 0.0) * dt_heads[:, :, None, :]
    mixing = (scores[:, None] * factor).astype(jnp.bfloat16)
    within = jnp.einsum(
        "gkts,sgkp->tgkp",
        mixing,
        x_half.reshape(length, G, heads_per, P_SIZE),
        preferred_element_type=jnp.float32,
    )
    weighted_c = state_reach(c_rows, cum_decay, span_count)
    from_state = jnp.einsum(
        "tgkn,gkpn->tgkp",
        weighted_c,
        state_in.reshape(G, heads_per, P_SIZE, N),
        precision=lax.Precision.HIGHEST,
    )
    skip_part = (
        x_rows.reshape(length, G, heads_per, P_SIZE)
        * skip_gain.reshape(G, heads_per)[None, :, :, None]
    )
    return (within + from_state + skip_part).reshape(length, H * P_SIZE).astype(jnp.bfloat16)


def join_flat(earlier, later):
    joined = []
    for member in range(0, len(earlier), 2):
        joined.append(earlier[member] * later[member])
        joined.append(later[member][:, None, None] * earlier[member + 1] + later[member + 1])
    return tuple(joined)


def fold_chain(rising, falling):
    identity = tuple(
        (
            jnp.ones_like(rising[member]) if member % 2 == 0 else jnp.zeros_like(rising[member])
            for member in range(len(rising))
        )
    )
    is_last = lax.axis_index("ctx") == lax.axis_size("ctx") - 1
    below = prefix(rising, "ctx", join_flat, identity, False)
    through = join_flat(below, rising)
    seeded_all = join_flat(through, falling)
    seeded = tuple(
        (jnp.where(is_last, seeded_all[member], falling[member]) for member in range(len(falling)))
    )
    above = prefix(seeded, "ctx", join_flat, identity, True)
    arriving = tuple(
        (jnp.where(is_last, through[member], above[member]) for member in range(len(above)))
    )
    return (below, arriving)


def shards(hidden_x, b_proj, c_proj, dt_raw, span_start, a_log, skip_gain, dt_bias, out_grad):
    x_rows = hidden_x.reshape(2, STRETCH, H * P_SIZE).astype(jnp.float32)
    b_rows = b_proj.reshape(2, STRETCH, G * N).astype(jnp.float32)
    c_rows = c_proj.reshape(2, STRETCH, G * N).astype(jnp.float32)
    dt_rows = dt_raw.reshape(2, STRETCH, H)
    starts = span_start.reshape(2, STRETCH)
    grads_in = out_grad.reshape(2, STRETCH, H * P_SIZE)
    summary_map = jax.vmap(stretch_summary, in_axes=(0, 0, 0, 0, None, None))
    output_map = jax.vmap(stretch_output, in_axes=(0, 0, 0, 0, 0, 0, None, None, None))

    def summarize(x_in, b_in, dt_in, rate_log, bias_in):
        return summary_map(x_in, b_in, dt_in, starts, rate_log, bias_in)

    (carried, local_sum), pull_summary = jax.vjp(summarize, x_rows, b_rows, dt_rows, a_log, dt_bias)
    below, arriving = fold_chain((carried[0], local_sum[0]), (carried[1], local_sum[1]))
    states = jnp.stack([below[1], arriving[1]])

    def with_state(x_in, b_in, c_in, dt_in, state_in, rate_log, gain_in, bias_in):
        return output_map(x_in, b_in, c_in, dt_in, starts, state_in, rate_log, gain_in, bias_in)

    mixed, pullback = jax.vjp(
        with_state, x_rows, b_rows, c_rows, dt_rows, states, a_log, skip_gain, dt_bias
    )
    grad_xo, grad_bo, grad_co, grad_dto, adjoint, grad_ao, grad_ko, grad_to = pullback(grads_in)
    back_below, back_arriving = fold_chain((carried[1], adjoint[1]), (carried[0], adjoint[0]))
    later_grad = jnp.stack([back_arriving[1], back_below[1]])
    rate_grad = jnp.sum(later_grad * states, axis=(2, 3))
    grad_xs, grad_bs, grad_dts, grad_as, grad_ts = pull_summary((rate_grad, later_grad))
    totals = lax.psum((grad_ao + grad_as, grad_ko, grad_to + grad_ts), ("dp", "ctx"))
    rows_here = 2 * STRETCH
    return (
        mixed.reshape(1, rows_here, H * P_SIZE),
        (grad_xo + grad_xs).reshape(1, rows_here, H * P_SIZE).astype(jnp.bfloat16),
        (grad_bo + grad_bs).reshape(1, rows_here, G * N).astype(jnp.bfloat16),
        grad_co.reshape(1, rows_here, G * N).astype(jnp.bfloat16),
        (grad_dto + grad_dts).reshape(1, rows_here, H),
        totals[0],
        totals[1],
        totals[2],
    )


def solution(mesh):
    return jax.shard_map(
        shards,
        mesh=mesh,
        in_specs=(
            P("dp", "ctx", None),
            P("dp", "ctx", None),
            P("dp", "ctx", None),
            P("dp", "ctx", None),
            P("dp", "ctx"),
            P(),
            P(),
            P(),
            P("dp", "ctx", None),
        ),
        out_specs=(
            P("dp", "ctx", None),
            P("dp", "ctx", None),
            P("dp", "ctx", None),
            P("dp", "ctx", None),
            P("dp", "ctx", None),
            P(),
            P(),
            P(),
        ),
        check_vma=False,
    )
```

profile of v0, /device:TPU:1, one launch (start us, length us, event | category | flops | bytes accessed | tf_op | source)
XLA Modules:
  0.0 1432.3 jit_solution(1084384336974843453)
XLA Ops:
  13.5 2.9 copy.243
  19.2 4.0 fusion.24
  25.0 3.1 copy.251
  30.3 6.3 fusion.41
  39.0 82.1 %all-gather.4 = f32[32,1,64]{2,1,0:T(1,128)S(1)} all-gather(f32[1,1,64]{2,1,0:T(1,128)S(1)} %get-tuple-element.710), channel_id=1, replica_groups=mesh['dp'=4,'ctx'=32] {'ctx'}, dimensions={0}, use_global_device_ids=true | all-gather | bytes 8448 | tf_op jit(solution)/shard_map/all_gather | solution.py:15
  121.1 75.6 %all-gather.5 = f32[32,1,64]{2,1,0:T(1,128)} all-gather(f32[1,1,64]{2,1,0:T(1,128)S(1)} %get-tuple-element.708), channel_id=1, replica_groups=mesh['dp'=4,'ctx'=32] {'ctx'}, dimensions={0}, use_global_device_ids=true | all-gather | bytes 8448 | tf_op jit(solution)/shard_map/all_gather | solution.py:15
  196.7 93.0 %all-gather.11.cloned.1.call-done = f32[32,64,32,64]{3,2,1,0:T(8,128)} async-done(((f32[1,64,32,64]{3,2,1,0:T(8,128)}), f32[32,64,32,64]{3,2,1,0:T(8,128)}) %all-gather.11.cloned.1.call-update) | async-done | bytes 16777232 | tf_op jit(solution)/shard_map/all_gather | solution.py:15
  289.7 49.8 %while.64 = (s32[]{:T(128)}, f32[64]{0:T(128)S(1)}, f32[64,32,64]{2,1,0:T(8,128)S(1)}, s32[]{:T(128)}, f32[32,64]{1,0:T(8,128)S(1)}, /*index=5*/f32[32,64,32,64]{3,2,1,0:T(8,128)}, s32[]{:T(128)}, s32[]{:T(128)}) while((s32[]{:T(128)}, f32[64]{0:T(128)S(1)}, f32[64,32,64]{2,1,0:T(8,128)S(1)}, s32[]{:T(128)}, ...), condition=%wide.region_5.7_spmd.clone, body=%wide.region_4.6_spmd.clone.sunk | while | flops 524484 | bytes 1574267 | solution.py:28
  339.5 212.4 %all-gather.13.cloned.1.call-done = f32[32,64,32,64]{3,2,1,0:T(8,128)} async-done(((f32[1,64,32,64]{3,2,1,0:T(8,128)}), f32[32,64,32,64]{3,2,1,0:T(8,128)}) %all-gather.13.cloned.1.call-update) | async-done | bytes 16777232 | tf_op jit(solution)/shard_map/all_gather | solution.py:15
  551.9 89.2 %while.66 = (s32[]{:T(128)}, f32[64]{0:T(128)}, f32[64,32,64]{2,1,0:T(8,128)S(1)}, s32[]{:T(128)}, f32[32,64]{1,0:T(8,128)}, /*index=5*/f32[32,64,32,64]{3,2,1,0:T(8,128)}, s32[]{:T(128)}, s32[]{:T(128)}) while((s32[]{:T(128)}, f32[64]{0:T(128)}, f32[64,32,64]{2,1,0:T(8,128)S(1)}, s32[]{:T(128)}, f32[32,64]{1,0:T(8,128)}, ...), condition=%wide.region_9.11_spmd.clone, body=%wide.region_8.10_spmd.clone.sunk | while | flops 524484 | bytes 1574267 | solution.py:28
  641.1 3.7 add_select_fusion
  655.7 2.8 fusion.64
  662.4 154.1 %all-reduce.6 = (f32[2048]{0:T(1024)}, f32[2048]{0:T(1024)}) all-reduce(f32[2048]{0:T(1024)} %fusion.81, f32[2048]{0:T(1024)} %fusion.82), channel_id=2, replica_groups=mesh['dp'=4,'ctx'=32] {'ctx'}, use_global_device_ids=true, to_apply=%add.3 | all-reduce | flops 4096 | bytes 32768
  819.3 88.6 %all-gather.17.cloned.1.call-done = f32[2048,32,64]{2,1,0:T(8,128)} async-done(((f32[64,32,64]{2,1,0:T(8,128)}), f32[2048,32,64]{2,1,0:T(8,128)}) %all-gather.17.cloned.1.call-update) | async-done | bytes 16777232 | tf_op jit(solution)/shard_map/all_gather | solution.py:15
  907.9 110.8 %while.67 = (s32[]{:T(128)}, f32[64,32,64]{2,1,0:T(8,128)}, s32[]{:T(128)}, f32[32,64]{1,0:T(8,128)}, f32[32,64,32,64]{3,2,1,0:T(8,128)}, /*index=5*/s32[]{:T(128)}, s32[]{:T(128)}, s32[]{:T(128)}, s32[]{:T(128)}) while((s32[]{:T(128)}, f32[64,32,64]{2,1,0:T(8,128)}, s32[]{:T(128)}, f32[32,64]{1,0:T(8,128)}, ...), condition=%wide.region_11.13_spmd.clone, body=%wide.region_10.12_spmd.clone.sunk | while | flops 524296 | bytes 1573807 | solution.py:28
  911.7 2.7 fusion.111
  915.1 2.7 fusion.111
  918.5 3.0 fusion.111
  922.2 2.7 fusion.111
  925.6 2.7 fusion.111
  929.0 2.8 fusion.111
  932.4 2.8 fusion.111
  935.9 2.7 fusion.111
  939.3 2.7 fusion.111
  942.7 2.7 fusion.111
  946.1 3.3 fusion.111
  950.2 2.7 fusion.111
  953.5 2.7 fusion.111
  957.0 2.7 fusion.111
  960.4 2.7 fusion.111
  963.8 2.7 fusion.111
  967.2 2.7 fusion.111
  970.6 2.7 fusion.111
  974.0 2.7 fusion.111
  977.4 2.7 fusion.111
  980.8 3.0 fusion.111
  984.5 2.7 fusion.111
  987.9 2.7 fusion.111
  991.3 2.7 fusion.111
  998.1 2.7 fusion.111
  1001.5 2.7 fusion.111
  1004.9 3.3 fusion.111
  1009.0 2.9 fusion.111
  1021.0 4.4 fusion.31
  1026.2 10.9 convert_bitcast_fusion
  1037.2 25.8 %fusion.14 = (f32[2,4,16,256]{3,2,1,0:T(8,128)}, f32[2,4,16,256]{3,2,1,0:T(8,128)}, f32[2,4,16,256]{3,2,1,0:T(8,128)}, bf16[2,4,256,256]{3,2,1,0:T(8,128)(2,1)}) fusion(f32[2,4,16,256]{3,2,1,0:T(8,128)S(1)} %bitcast.324, f32[2,256,256]{2,1,0:T(8,128)S(1)} %copy-done.26, f32[2,4,16,256]{3,2,1,0:T(8,128)S(1)} %copy-done.31, ...), kind=kOutput, calls=%fused_computation.30 | convolution fusion | flops 678854656 | bytes 8650752 | tf_op jit(solution)/shard_map/transpose(jvp(vmap(gkts,sgkp->tgkp)))/dot_general | solution.py:90
  1063.0 107.0 %all-gather.15.cloned.1.call-done = f32[2048,32,64]{2,1,0:T(8,128)} async-done(((f32[64,32,64]{2,1,0:T(8,128)}), f32[2048,32,64]{2,1,0:T(8,128)}) %all-gather.15.cloned.1.call-update) | async-done | bytes 16777232 | tf_op jit(solution)/shard_map/all_gather | solution.py:15
  1170.0 70.7 %while.65 = (s32[]{:T(128)}, f32[64,32,64]{2,1,0:T(8,128)S(1)}, s32[]{:T(128)}, f32[32,64]{1,0:T(8,128)}, f32[32,64,32,64]{3,2,1,0:T(8,128)}, /*index=5*/s32[]{:T(128)}, s32[]{:T(128)}, s32[]{:T(128)}, s32[]{:T(128)}) while((s32[]{:T(128)}, f32[64,32,64]{2,1,0:T(8,128)S(1)}, s32[]{:T(128)}, f32[32,64]{1,0:T(8,128)}, ...), condition=%wide.region_7.9_spmd.clone, body=%wide.region_6.8_spmd.clone.sunk | while | flops 524296 | bytes 1573807 | solution.py:28
  1242.3 5.8 fusion.17
  1248.2 6.0 fusion.22
  1254.2 10.9 fusion.30
  1265.1 3.5 copy.250
  1268.6 4.4 convert_element_type.144
  1273.0 3.9 copy.276
  1276.9 8.1 copy.257
  1285.0 6.4 reshape.473
  1291.4 8.1 copy.254
  1299.5 6.6 reshape.484
  1306.1 7.1 fusion.28
  1313.3 4.0 copy.277
  1318.8 6.1 fusion.50
  1345.8 5.0 reduce-window.36
  1353.0 5.0 reduce-window.34
  1360.9 64.5 %all-reduce.5 = (f32[64]{0:T(128)}, f32[64]{0:T(128)}, f32[64]{0:T(128)}) all-reduce(f32[64]{0:T(128)S(1)} %add_multiply_fusion, f32[64]{0:T(128)S(1)} %reshape.483, f32[64]{0:T(128)S(1)} %add.223), channel_id=1, replica_groups=mesh['dp'=4,'ctx'=32] {'dp','ctx'}, use_global_device_ids=true, to_apply=%region_27.29 | all-reduce | flops 192 | bytes 1536 | tf_op jit(solution)/shard_map/psum | solution.py:167
  (421 shorter events, 303.2 us)
Async XLA Ops:
  7.2 282.5 %all-gather.11.cloned.1.call-start = ((), (), s32[]{:S(2)}) async-start(), calls=%async_computation | async-start | bytes 34603008 | tf_op jit(solution)/shard_map/all_gather | solution.py:15
  9.2 9.7 copy-start.39
  9.9 3.4 copy-start.46
  10.9 8.0 copy-start.11
  13.3 3.1 copy-start.28
  13.5 5.2 copy-start.29
  13.5 5.5 copy-start.44
  16.4 6.7 copy-start
  18.9 5.8 copy-start.8
  19.1 5.5 copy-start.22
  19.2 11.2 copy-start.24
  19.2 5.6 copy-start.30
  24.7 527.2 %all-gather.13.cloned.1.call-start = ((), (), s32[]{:S(2)}) async-start(), calls=%async_computation.1 | async-start | bytes 34603008 | tf_op jit(solution)/shard_map/all_gather | solution.py:15
  25.0 5.3 copy-start.18
  28.1 8.5 copy-start.1
  38.2 869.7 %all-gather.17.cloned.1.call-start = ((), (), s32[]{:S(2)}) async-start(), calls=%async_computation.3 | async-start | bytes 34603008 | tf_op jit(solution)/shard_map/all_gather | solution.py:15
  38.3 251.4 %copy-start.47 = (pred[2]{0:T(512)(128)(4,1)}, pred[2]{0:T(512)(128)(4,1)S(1)}, u32[]{:S(2)}) copy-start(pred[2]{0:T(512)(128)(4,1)S(1)} %broadcast_compare_fusion) | copy-start | bytes 10
  38.4 251.3 %copy-start.42 = (f32[2,64]{1,0:T(2,128)}, f32[2,64]{1,0:T(2,128)S(1)}, u32[]{:S(2)}) copy-start(f32[2,64]{1,0:T(2,128)S(1)} %multiply_select_fusion) | copy-start | bytes 1540
  339.4 212.4 %copy-start.41 = (f32[64]{0:T(128)}, f32[64]{0:T(128)S(1)}, u32[]{:S(2)}) copy-start(f32[64]{0:T(128)S(1)} %get-tuple-element.496) | copy-start | bytes 772
  551.9 89.2 %copy-start.2 = (f32[1,4,16,32,64]{4,3,2,1,0:T(8,128)S(1)}, f32[1,4,16,32,64]{4,3,2,1,0:T(8,128)}, u32[]{:S(2)}) copy-start(f32[1,4,16,32,64]{4,3,2,1,0:T(8,128)} %get-tuple-element.692) | copy-start | bytes 1572868
  644.8 525.1 %all-gather.15.cloned.1.call-start = ((), (), s32[]{:S(2)}) async-start(), calls=%async_computation.2 | async-start | bytes 34603008 | tf_op jit(solution)/shard_map/all_gather | solution.py:15
  1018.7 2.2 copy-start.6
  1018.7 2.2 copy-start.9
  1018.7 2.2 copy-start.23
  1020.6 4.8 copy-start.3
  1020.9 4.4 copy-start.12
  1020.9 4.4 copy-start.45
  1020.9 5.2 copy-start.14
  1020.9 5.2 copy-start.16
  1021.0 5.2 copy-start.26
  1021.0 5.2 copy-start.31
  1021.0 5.2 copy-start.33
  1025.4 0.8 copy-start.20
  1026.2 11.0 copy-start.35
  1240.7 1.5 copy-start.19
  1240.7 1.5 copy-start.25
  1242.2 12.0 copy-start.5
  1242.2 5.9 copy-start.17
  1248.1 6.1 copy-start.7
  1248.1 6.1 copy-start.15
  1248.1 6.0 copy-start.27
  1248.1 6.0 copy-start.32
  1248.2 6.0 copy-start.34
  1248.2 6.0 copy-start.36
  1248.2 6.0 copy-start.43
  1299.5 6.6 copy-start.37
  1313.3 5.5 copy-start.4
  1318.8 10.3 copy-start.10
  1331.6 20.4 %copy-start.40 = (f32[2,256]{1,0:T(2,128)S(1)}, f32[2,256]{1,0:T(2,128)}, u32[]{:S(2)}) copy-start(f32[2,256]{1,0:T(2,128)} %copy-done.39) | copy-start | bytes 6148
  1333.6 24.8 %copy-start.13 = (f32[2,256,64]{1,0,2:T(2,128)S(1)}, f32[2,256,64]{1,0,2:T(2,128)}, u32[]{:S(2)}) copy-start(f32[2,256,64]{1,0,2:T(2,128)} %copy-done.11) | copy-start | bytes 393220
  1333.6 24.8 %copy-start.21 = (f32[2,256,4,16]{1,3,2,0:T(8,128)S(1)}, f32[2,256,4,16]{1,3,2,0:T(8,128)}, u32[]{:S(2)}) copy-start(f32[2,256,4,16]{1,3,2,0:T(8,128)} %copy-done.20) | copy-start | bytes 393220
  1343.0 17.7 %copy-start.38 = (f32[2048]{0:T(1024)S(1)}, f32[2048]{0:T(1024)}, u32[]{:S(2)}) copy-start(f32[2048]{0:T(1024)} %get-tuple-element.687) | copy-start | bytes 24580
  1343.0 17.9 %copy-start.48 = (f32[64]{0:T(128)S(1)}, f32[64]{0:T(128)}, u32[]{:S(2)}) copy-start(f32[64]{0:T(128)} %param.23) | copy-start | bytes 772
Sparse Core Ops, SparseCore 0:
  24.8 264.8 all-gather.10
  292.7 259.1 all-gather.12
  645.0 262.9 all-gather.16
  910.8 259.1 all-gather.14
where the time goes:
time: 1450 us; the launch traced here: 1430 us
  waiting for transfers between devices  501 us (35%)
  blocking collectives  376 us (26%)
  other arithmetic  317 us (22%)
  local copies, waits for them, and re-layouts  131 us (9%)
  matrix products  87 us (6%)
  between operations  15.6 us (1%)
    all_gather x4, waiting for transfers between devices, prefix(): everything = jax.tree.map(lambda part: lax.all_gather(part, axis), array)  501 us
    select_n x192, other arithmetic, lap(): return jax.tree.map(lambda a, b: jnp.where(reached, a, b), new, before)  273 us
    all_gather x2, blocking collectives, prefix(): everything = jax.tree.map(lambda part: lax.all_gather(part, axis), array)  158 us
    unnamed x1, blocking collectives  154 us
    psum x1, blocking collectives, shards(): lax.psum((grad_ao + grad_as, grad_ko, grad_to + grad_ts), ('dp', 'ctx'))  64.5 us
    dot_general x3, matrix products, stretch_output(): jnp.einsum('gkts,sgkp->tgkp', mixing, x_half.reshape(length, G, heads_per...  47.6 us
    mul x65, local copies, waits for them, and re-layouts, join_flat(): later[member][:, None, None] * earlier[member + 1] + later[member + 1]  44.8 us
  transfers between devices with their start and end apart: 4, of which 4 were waited for; matrix products, arithmetic and copies ran while one was open for 17% of the time, Pallas kernels for 0%

commit v1 on v0

v1 whole, which is shorter than its diff:
```python
import functools

import jax
import jax.numpy as jnp
from jax import lax
from jax.experimental import pallas as pl
from jax.experimental.pallas import tpu as pltpu
from jax.sharding import PartitionSpec as P

H = 64
P_SIZE = 32
N = 64
G = 4
STRETCH = 256
ROWS = 2 * STRETCH
WIDTH = H * P_SIZE
GROUP = WIDTH // G
STEPS = 2
STEP_W = WIDTH // STEPS
STEP_N = G * N // STEPS
XY = 16
LANES = WIDTH // XY
CHUNKS = 4
CH = N // CHUNKS
F32 = jnp.float32
BF16 = jnp.bfloat16
MESH = pl.DeviceIdType.MESH
NN = ((1,), (0,))
NT = ((1,), (1,))
TN = ((0,), (0,))


def dot(a, b, dims=NN, precision=None):
    return lax.dot_general(a, b, (dims, ((), ())), preferred_element_type=F32, precision=precision)


def split(a):
    high = a.astype(BF16)
    return high, (a - high.astype(F32)).astype(BF16)


def head_map(step):
    head = lax.broadcasted_iota(jnp.int32, (H, STEP_W), 0)
    column = lax.broadcasted_iota(jnp.int32, (H, STEP_W), 1) + step * STEP_W
    return jnp.where(column // P_SIZE == head, 1.0, 0.0).astype(BF16)


def triangle(lower):
    row = lax.broadcasted_iota(jnp.int32, (STRETCH, STRETCH), 0)
    column = lax.broadcasted_iota(jnp.int32, (STRETCH, STRETCH), 1)
    return jnp.where(row >= column if lower else row <= column, 1.0, 0.0)


def decay_terms(dt_raw, a_log, dt_bias):
    shifted = dt_raw + dt_bias
    small = jnp.exp(-jnp.abs(shifted))
    dt = jnp.maximum(shifted, 0.0) + jnp.log1p(small)
    running = dot(triangle(True), dt, precision=lax.Precision.HIGHEST)
    return shifted, dt, -jnp.exp(a_log) * running


def counts(start_row):
    start = jnp.broadcast_to(start_row.astype(F32), (8, STRETCH)).astype(BF16)
    low = triangle(True).astype(BF16)
    return dot(low, start, NT)[:, :1], dot(start, low, NT)[:1]


def summary_kernel(x_ref, go_ref, b_ref, c_ref, dt_ref, start_ref, al_ref, tb_ref, part_ref, decay_ref, u_s, v_s, m_s):
    step = pl.program_id(0)

    @pl.when(step == 0)
    def _():
        for block in range(2):
            rows = pl.ds(block * STRETCH, STRETCH)
            _, dt, cum = decay_terms(dt_ref[rows], al_ref[...], tb_ref[...])
            u_s[rows] = jnp.concatenate(split(jnp.exp(cum)), axis=1)
            v_s[rows] = jnp.concatenate(split(jnp.exp(-cum) * dt), axis=1)
            column, _ = counts(start_ref[:, block * STRETCH : (block + 1) * STRETCH])
            last = column[STRETCH - 1 :]
            enters = jnp.where(column == 0.0, 1.0, 0.0)
            stays = jnp.where(column == last, 1.0, 0.0)
            m_s[rows] = jnp.concatenate(
                [jnp.broadcast_to(enters, (STRETCH, N)), jnp.broadcast_to(stays, (STRETCH, N))], axis=1
            )

    heads = head_map(step)
    heads = jnp.concatenate([heads, heads], axis=0)
    decays = []
    for block in range(2):
        rows = pl.ds(block * STRETCH, STRETCH)
        mask = m_s[rows]
        enters, stays = mask[:, :N], mask[:, N:]
        for group in range(G // STEPS):
            cols = pl.ds(group * GROUP, GROUP)
            expand = heads[:, group * GROUP : (group + 1) * GROUP]
            u = dot(u_s[rows], expand)
            v = dot(v_s[rows], expand)
            total = u[STRETCH - 1 :]
            scaled_x = (x_ref[rows, cols].astype(F32) * (v * total)).astype(BF16)
            scaled_g = (go_ref[rows, cols].astype(F32) * u).astype(BF16)
            b_in = b_ref[rows, group * N : (group + 1) * N]
            c_in = c_ref[rows, group * N : (group + 1) * N]
            b_in = (b_in.astype(F32) * stays).astype(BF16)
            c_in = (c_in.astype(F32) * enters).astype(BF16)
            part_ref[0, block, :, cols] = dot(b_in, scaled_x, TN)
            part_ref[1, 1 - block, :, cols] = dot(c_in, scaled_g, TN)
            kept = jnp.broadcast_to(enters[STRETCH - 1 :, :1], (1, GROUP))
            decays.append(total * kept)
    first = jnp.concatenate(decays[: G // STEPS], axis=1)
    second = jnp.concatenate(decays[G // STEPS :], axis=1)
    row = lax.broadcasted_iota(jnp.int32, (8, STEP_W), 0)
    decay_ref[...] = jnp.where(row == 0, first, jnp.where(row == 1, second, 0.0))


def chain_kernel(part, decay, state, z_in, z_decay, up, up_in, down, down_in, z_out, z_s, z_r, up_s, up_r, down_s, down_r, back_s, back_r):
    here = lax.axis_index("ctx")
    side, place = lax.rem(here, 2), here // 2
    partner = {"ctx": here + 1 - 2 * side}

    def peer(k):
        return lax.rem(place + k, XY)

    def device(k):
        return {"ctx": peer(k) * 2 + side}

    barrier = pltpu.get_barrier_semaphore()
    pl.semaphore_signal(barrier, inc=1, device_id=partner, device_id_type=MESH)

    def greet(k, carry):
        pl.semaphore_signal(barrier, inc=1, device_id=device(k), device_id_type=MESH)
        return carry

    lax.fori_loop(1, XY, greet, 0)
    pl.semaphore_wait(barrier, XY)

    def remote(src, dst, send, recv, to):
        return pltpu.make_async_remote_copy(
            src_ref=src, dst_ref=dst, send_sem=send, recv_sem=recv, device_id=to, device_id_type=MESH
        )

    def z_up(q):
        rows = pl.ds(q * CH, CH)
        return remote(part.at[1 - side, :, rows], z_in.at[:, rows], z_s.at[q], z_r.at[q], partner)

    z_decays = remote(decay, z_decay, z_s.at[CHUNKS], z_r.at[CHUNKS], partner)
    z_decays.start()
    for q in range(CHUNKS):
        z_up(q).start()

    def up_rows(q):
        return pl.ds(8 + q * 2 * CH, 2 * CH) if q else pl.ds(0, 8 + 2 * CH)

    def up_copy(q, k):
        return remote(up.at[peer(k), up_rows(q)], up_in.at[place, up_rows(q)], up_s.at[q, k], up_r.at[q, k], device(k))

    def down_rows(q):
        return pl.ds(q * 2 * CH, 2 * CH)

    def down_copy(q, k):
        return remote(down.at[peer(k), down_rows(q)], down_in.at[place, down_rows(q)], down_s.at[q, k], down_r.at[q, k], device(k))

    def z_back(q):
        rows = pl.ds(q * CH, CH)
        return remote(z_out.at[:, rows], state.at[side, :, rows], back_s.at[q], back_r.at[q], partner)

    z_decays.wait_recv()
    at_zero = side == 0
    mine = [jnp.where(at_zero, decay[s : s + 1], decay[1 - s : 2 - s]) for s in range(2)]
    theirs = [jnp.where(at_zero, z_decay[s : s + 1], z_decay[1 - s : 2 - s]) for s in range(2)]
    first = [at_zero, jnp.logical_not(at_zero)]

    for q in range(CHUNKS):
        rows = pl.ds(q * CH, CH)
        z_up(q).wait_recv()
        if q == 0:
            pair = [mine[s] * theirs[s] for s in range(2)]
            row = lax.broadcasted_iota(jnp.int32, (8, LANES), 0)
            for o in range(XY):
                lanes = slice(o * LANES, (o + 1) * LANES)
                up[o, :8] = jnp.where(row == 0, pair[0][:, lanes], jnp.where(row == 1, pair[1][:, lanes], 0.0))
        for s in range(2):
            scale_mine = jnp.where(first[s], theirs[s], 1.0)
            scale_theirs = jnp.where(first[s], 1.0, mine[s])
            total = scale_mine * part[side, s, rows] + scale_theirs * z_in[s, rows]
            for o in range(XY):
                up[o, pl.ds(8 + (2 * q + s) * CH, CH)] = total[:, o * LANES : (o + 1) * LANES]

        def send_up(k, carry):
            up_copy(q, k).start()
            return carry

        lax.fori_loop(1, XY, send_up, 0)
        up_in[place, up_rows(q)] = up[place, up_rows(q)]

    for q in range(CHUNKS):

        def await_up(k, carry):
            up_copy(q, k).wait_recv()
            return carry

        lax.fori_loop(1, XY, await_up, 0)

        def rise(j, now):
            down[j, pl.ds(2 * q * CH, CH)] = now
            return up_in[j, 0:1] * now + up_in[j, pl.ds(8 + 2 * q * CH, CH)]

        def fall(k, now):
            j = XY - 1 - k
            down[j, pl.ds((2 * q + 1) * CH, CH)] = now
            return up_in[j, 1:2] * now + up_in[j, pl.ds(8 + (2 * q + 1) * CH, CH)]

        now = lax.fori_loop(0, XY, rise, jnp.zeros((CH, LANES), F32))
        lax.fori_loop(0, XY, fall, now)

        def send_down(k, carry):
            down_copy(q, k).start()
            return carry

        lax.fori_loop(1, XY, send_down, 0)
        down_in[place, down_rows(q)] = down[place, down_rows(q)]

    for q in range(CHUNKS):
        rows = pl.ds(q * CH, CH)

        def await_down(k, carry):
            down_copy(q, k).wait_recv()
            return carry

        lax.fori_loop(1, XY, await_down, 0)
        for s in range(2):
            keep = jnp.where(first[s], 1.0, theirs[s])
            keep_add = jnp.where(first[s], 0.0, 1.0)
            give = jnp.where(first[s], mine[s], 1.0)
            give_add = jnp.where(first[s], 1.0, 0.0)
            enter = jnp.concatenate([down_in[o, pl.ds((2 * q + s) * CH, CH)] for o in range(XY)], axis=1)
            state[side, s, rows] = keep * enter + keep_add * z_in[s, rows]
            z_out[s, rows] = give * enter + give_add * part[side, s, rows]
        z_back(q).start()

    for q in range(CHUNKS):
        z_back(q).wait()
        z_up(q).wait_send()

        def await_sent(k, carry):
            up_copy(q, k).wait_send()
            down_copy(q, k).wait_send()
            return carry

        lax.fori_loop(1, XY, await_sent, 0)
    z_decays.wait_send()


def output_kernel(x_ref, go_ref, b_ref, c_ref, dt_ref, start_ref, al_ref, sk_ref, tb_ref, state_ref, mixed_ref, gx_ref, gb_ref, gc_ref, gdt_ref, params_ref, u_s, v_s, m_s, cum_s, seen_s, seen_t, net_s, late_s, end_s, skip_s):
    step = pl.program_id(0)

    @pl.when(step == 0)
    def _():
        for block in range(2):
            rows = pl.ds(block * STRETCH, STRETCH)
            _, dt, cum = decay_terms(dt_ref[rows], al_ref[...], tb_ref[...])
            cum_s[rows] = cum
            u_s[rows] = jnp.concatenate(split(jnp.exp(cum)), axis=1)
            v_s[rows] = jnp.concatenate(split(jnp.exp(-cum) * dt), axis=1)
            column, row = counts(start_ref[:, block * STRETCH : (block + 1) * STRETCH])
            last = column[STRETCH - 1 :]
            enters = jnp.where(column == 0.0, 1.0, 0.0)
            stays = jnp.where(column == last, 1.0, 0.0)
            m_s[rows] = jnp.concatenate(
                [jnp.broadcast_to(enters, (STRETCH, N)), jnp.broadcast_to(stays, (STRETCH, N))], axis=1
            )
            same = jnp.where(column == row, 1.0, 0.0)
            seen_s[rows] = same * triangle(True)
            seen_t[rows] = same * triangle(False)
        net_s[...] = jnp.zeros_like(net_s)
        late_s[...] = jnp.zeros_like(late_s)
        end_s[...] = jnp.zeros_like(end_s)
        skip_s[...] = jnp.zeros_like(skip_s)

    heads = head_map(step)
    twice = jnp.concatenate([heads, heads], axis=0)
    skip_row = dot(jnp.concatenate(split(jnp.broadcast_to(sk_ref[...], (8, H))), axis=1), twice)[:1]

    def by_head(values, where):
        high, low = split(values)
        return dot(high, where, NT) + dot(low, where, NT)

    for block in range(2):
        rows = pl.ds(block * STRETCH, STRETCH)
        mask = m_s[rows]
        enters, stays = mask[:, :N], mask[:, N:]
        seen, seen_back = seen_s[rows], seen_t[rows]
        for group in range(G // STEPS):
            cols = pl.ds(group * GROUP, GROUP)
            lanes = slice(group * GROUP, (group + 1) * GROUP)
            where = heads[:, lanes]
            expand = twice[:, lanes]
            u = dot(u_s[rows], expand)
            v = dot(v_s[rows], expand)
            total = u[STRETCH - 1 :]
            x = x_ref[rows, cols].astype(F32)
            go = go_ref[rows, cols].astype(F32)
            xv = (x * v).astype(BF16)
            gu = (go * u).astype(BF16)
            xk = (x * (v * total)).astype(BF16)
            narrow = slice(group * N, (group + 1) * N)
            b_in, c_in = b_ref[rows, narrow], c_ref[rows, narrow]
            b_stay = (b_in.astype(F32) * stays).astype(BF16)
            c_enter = (c_in.astype(F32) * enters).astype(BF16)
            entering = state_ref[0, block, :, cols]
            later = state_ref[1, 1 - block, :, cols]
            entering_half, later_half = entering.astype(BF16), later.astype(BF16)
            scores = (dot(c_in, b_in, NT) * seen).astype(BF16)
            scores_back = (dot(b_in, c_in, NT) * seen_back).astype(BF16)
            y = dot(scores, xv) + dot(c_enter, entering_half)
            from_later = total * dot(b_stay, later_half)
            z = dot(scores_back, gu) + from_later
            skip = skip_row[:, lanes]
            mixed_ref[rows, cols] = (u * y + skip * x).astype(BF16)
            gx_ref[rows, cols] = (v * z + skip * go).astype(BF16)
            grad_scores = jnp.where(seen > 0.0, dot(gu, xv, NT), 0.0).astype(BF16)
            gc_ref[rows, narrow] = (dot(grad_scores, b_in) + enters * dot(gu, entering_half, NT)).astype(BF16)
            gb_ref[rows, narrow] = (dot(grad_scores, c_in, TN) + stays * dot(xk, later_half, NT)).astype(BF16)
            xv_wide = xv.astype(F32)
            from_z = xv_wide * z
            net_s[rows] += by_head(gu.astype(F32) * y - from_z, where)
            late_s[rows] += by_head(from_z, where)
            kept = jnp.broadcast_to(enters[STRETCH - 1 :, :1], (1, GROUP))
            ends = jnp.sum(xv_wide * from_later, axis=0, keepdims=True)
            ends += total * kept * jnp.sum(entering * later, axis=0, keepdims=True)
            end_s[block * 8 : (block + 1) * 8] += by_head(jnp.broadcast_to(ends, (8, GROUP)), where)
            skips = jnp.sum(x * go, axis=0, keepdims=True)
            skip_s[...] += by_head(jnp.broadcast_to(skips, (8, GROUP)), where)

    @pl.when(step == STEPS - 1)
    def _():
        rate = -jnp.exp(al_ref[...])
        grad_a = jnp.zeros((1, H), F32)
        grad_t = jnp.zeros((1, H), F32)
        position = lax.broadcasted_iota(jnp.int32, (STRETCH, H), 0)
        for block in range(2):
            rows = pl.ds(block * STRETCH, STRETCH)
            shifted = dt_ref[rows] + tb_ref[...]
            small = jnp.exp(-jnp.abs(shifted))
            dt = jnp.maximum(shifted, 0.0) + jnp.log1p(small)
            slope = jnp.where(shifted >= 0.0, 1.0, small) / (1.0 + small)
            grad_cum = net_s[rows] + jnp.where(position == STRETCH - 1, end_s[block * 8 : block * 8 + 1], 0.0)
            after = dot(triangle(False), grad_cum, precision=lax.Precision.HIGHEST)
            grad_dt = (late_s[rows] / dt + rate * after) * slope
            gdt_ref[rows] = grad_dt
            grad_a += jnp.sum(cum_s[rows] * grad_cum, axis=0, keepdims=True)
            grad_t += jnp.sum(grad_dt, axis=0, keepdims=True)
        row = lax.broadcasted_iota(jnp.int32, (8, H), 0)
        params_ref[...] = jnp.where(row == 0, grad_a, jnp.where(row == 1, skip_s[:1], jnp.where(row == 2, grad_t, 0.0)))


def total_kernel(x, a_ref, k_ref, t_ref, buf1, buf2, s1, r1, s2, r2):
    here, dp = lax.axis_index("ctx"), lax.axis_index("dp")
    side, place = lax.rem(here, 2), here // 2
    mine = dp * 2 + side

    def near(k):
        return {"ctx": lax.rem(place + k, XY) * 2 + side}

    def far(k):
        g = lax.rem(mine + k, 8)
        return {"dp": g // 2, "ctx": place * 2 + lax.rem(g, 2)}

    barrier = pltpu.get_barrier_semaphore()
    for k in range(1, XY):
        pl.semaphore_signal(barrier, inc=1, device_id=near(k), device_id_type=MESH)
    for k in range(1, 8):
        pl.semaphore_signal(barrier, inc=1, device_id=far(k), device_id_type=MESH)
    pl.semaphore_wait(barrier, XY + 6)

    def exchange(src, buf, send, recv, to, count):
        copies = []
        for k in range(1, count):
            copy = pltpu.make_async_remote_copy(
                src_ref=src, dst_ref=buf.at[k], send_sem=send.at[k], recv_sem=recv.at[k], device_id=to(k), device_id_type=MESH
            )
            copy.start()
            copies.append(copy)
        for copy in copies:
            copy.wait()

    buf1[0] = x[...]
    exchange(x, buf1, s1, r1, near, XY)
    buf2[0] = jnp.sum(buf1[...], axis=0)
    exchange(buf2.at[0], buf2, s2, r2, far, 8)
    total = jnp.zeros((8, H), F32)
    for g in range(8):
        total += buf2[lax.rem(g - mine + 8, 8)]
    a_ref[...] = total[0:1]
    k_ref[...] = total[1:2]
    t_ref[...] = total[2:3]


def shards(hidden_x, b_proj, c_proj, dt_raw, span_start, a_log, skip_gain, dt_bias, out_grad):
    x = hidden_x.reshape(ROWS, WIDTH)
    go = out_grad.reshape(ROWS, WIDTH)
    b = b_proj.reshape(ROWS, G * N)
    c = c_proj.reshape(ROWS, G * N)
    dt = dt_raw.reshape(ROWS, H)
    start = span_start.reshape(1, ROWS)
    al, sk, tb = a_log.reshape(1, H), skip_gain.reshape(1, H), dt_bias.reshape(1, H)

    wide = pl.BlockSpec((ROWS, STEP_W), lambda i: (0, i))
    narrow = pl.BlockSpec((ROWS, STEP_N), lambda i: (0, i))

    def whole(*shape):
        return pl.BlockSpec(shape, lambda i: (0,) * len(shape))

    vmem = pl.BlockSpec(memory_space=pltpu.VMEM)
    part, decay = pl.pallas_call(
        summary_kernel,
        grid=(STEPS,),
        out_shape=(jax.ShapeDtypeStruct((2, 2, N, WIDTH), F32), jax.ShapeDtypeStruct((8, WIDTH), F32)),
        in_specs=[wide, wide, narrow, narrow, whole(ROWS, H), whole(1, ROWS), whole(1, H), whole(1, H)],
        out_specs=(
            pl.BlockSpec((2, 2, N, STEP_W), lambda i: (0, 0, 0, i)),
            pl.BlockSpec((8, STEP_W), lambda i: (0, i)),
        ),
        scratch_shapes=[
            pltpu.VMEM((ROWS, 2 * H), BF16),
            pltpu.VMEM((ROWS, 2 * H), BF16),
            pltpu.VMEM((ROWS, 2 * N), F32),
        ],
        compiler_params=pltpu.CompilerParams(vmem_limit_bytes=48 * 2**20),
        cost_estimate=pl.CostEstimate(flops=10**9, bytes_accessed=8 * 2**20, transcendentals=10**5),
        name="summary",
    )(x, go, b, c, dt, start, al, tb)

    dma = pltpu.SemaphoreType.DMA
    state = pl.pallas_call(
        chain_kernel,
        out_shape=jax.ShapeDtypeStruct((2, 2, N, WIDTH), F32),
        in_specs=[vmem, vmem],
        out_specs=vmem,
        scratch_shapes=[
            pltpu.VMEM((2, N, WIDTH), F32),
            pltpu.VMEM((8, WIDTH), F32),
            pltpu.VMEM((XY, 8 + 2 * N, LANES), F32),
            pltpu.VMEM((XY, 8 + 2 * N, LANES), F32),
            pltpu.VMEM((XY, 2 * N, LANES), F32),
            pltpu.VMEM((XY, 2 * N, LANES), F32),
            pltpu.VMEM((2, N, WIDTH), F32),
            dma((CHUNKS + 1,)),
            dma((CHUNKS + 1,)),
            dma((CHUNKS, XY)),
            dma((CHUNKS, XY)),
            dma((CHUNKS, XY)),
            dma((CHUNKS, XY)),
            dma((CHUNKS,)),
            dma((CHUNKS,)),
        ],
        compiler_params=pltpu.CompilerParams(
            collective_id=0, has_side_effects=True, vmem_limit_bytes=48 * 2**20
        ),
        name="chain",
    )(part, decay)

    half = jax.ShapeDtypeStruct((ROWS, WIDTH), BF16)
    slim = jax.ShapeDtypeStruct((ROWS, G * N), BF16)
    mixed, gx, gb, gc, gdt, params = pl.pallas_call(
        output_kernel,
        grid=(STEPS,),
        out_shape=(half, half, slim, slim, jax.ShapeDtypeStruct((ROWS, H), F32), jax.ShapeDtypeStruct((8, H), F32)),
        in_specs=[wide, wide, narrow, narrow, whole(ROWS, H), whole(1, ROWS), whole(1, H), whole(1, H), whole(1, H),
                  pl.BlockSpec((2, 2, N, STEP_W), lambda i: (0, 0, 0, i))],
        out_specs=(wide, wide, narrow, narrow, whole(ROWS, H), whole(8, H)),
        scratch_shapes=[
            pltpu.VMEM((ROWS, 2 * H), BF16),
            pltpu.VMEM((ROWS, 2 * H), BF16),
            pltpu.VMEM((ROWS, 2 * N), F32),
            pltpu.VMEM((ROWS, H), F32),
            pltpu.VMEM((ROWS, STRETCH), F32),
            pltpu.VMEM((ROWS, STRETCH), F32),
            pltpu.VMEM((ROWS, H), F32),
            pltpu.VMEM((ROWS, H), F32),
            pltpu.VMEM((16, H), F32),
            pltpu.VMEM((8, H), F32),
        ],
        compiler_params=pltpu.CompilerParams(vmem_limit_bytes=48 * 2**20),
        cost_estimate=pl.CostEstimate(flops=4 * 10**9, bytes_accessed=12 * 2**20, transcendentals=10**5),
        name="outputs",
    )(x, go, b, c, dt, start, al, sk, tb, state)

    line = jax.ShapeDtypeStruct((1, H), F32)
    grad_a, grad_k, grad_t = pl.pallas_call(
        total_kernel,
        out_shape=(line, line, line),
        in_specs=[vmem],
        out_specs=(vmem, vmem, vmem),
        scratch_shapes=[pltpu.VMEM((XY, 8, H), F32), pltpu.VMEM((8, 8, H), F32), dma((XY,)), dma((XY,)), dma((8,)), dma((8,))],
        compiler_params=pltpu.CompilerParams(collective_id=1, has_side_effects=True),
        name="totals",
    )(params)
    return (
        mixed.reshape(1, ROWS, WIDTH),
        gx.reshape(1, ROWS, WIDTH),
        gb.reshape(1, ROWS, G * N),
        gc.reshape(1, ROWS, G * N),
        gdt.reshape(1, ROWS, H),
        grad_a.reshape(H),
        grad_k.reshape(H),
        grad_t.reshape(H),
    )


def solution(mesh):
    rows = P("dp", "ctx", None)
    return jax.shard_map(
        shards,
        mesh=mesh,
        in_specs=(rows, rows, rows, rows, P("dp", "ctx"), P(), P(), P(), rows),
        out_specs=(rows, rows, rows, rows, rows, P(), P(), P()),
        check_vma=False,
    )
```

time: 1450 us -> 119 us (0.08); the launches traced: 1430 us -> 118 us
  waiting for transfers between devices: 501 us -> 0 us
  blocking collectives: 376 us -> 0 us
  other arithmetic: 317 us -> 0 us
  local copies, waits for them, and re-layouts: 131 us -> 12.6 us
  Pallas kernels: 0 us -> 105 us
  matrix products: 87 us -> 0 us
  between operations: 15.6 us -> 0.73 us
    all_gather x4 -> x0, waiting for transfers between devices: 501 us -> none  [prefix(): everything = jax.tree.map(lambda part: lax.all_gather(part, axis), array)]
    select_n x198 -> x0, other arithmetic: 281 us -> none  [the longest x192 273 us: lap(): return jax.tree.map(lambda a, b: jnp.where(reached, a, b), new, before)]
    all_gather x2 -> x0, blocking collectives: 158 us -> none  [prefix(): everything = jax.tree.map(lambda part: lax.all_gather(part, axis), array)]
    unnamed x1 -> x0, blocking collectives: 154 us -> none
    pallas_call x0 -> x4, Pallas kernels: none -> 105 us  [the longest x1 62.7 us: shards(): pl.pallas_call(chain_kernel, out_shape=jax.ShapeDtypeStruct((2, 2, N, WID...]
    dot_general x12 -> x0, matrix products: 87 us -> none  [the longest x3 47.6 us: stretch_output(): jnp.einsum('gkts,sgkp->tgkp', mixing, x_half.reshape(length, G, heads_per...]
    psum x1 -> x0, blocking collectives: 64.5 us -> none  [shards(): lax.psum((grad_ao + grad_as, grad_ko, grad_to + grad_ts), ('dp', 'ctx'))]
    mul x69 -> x0, local copies, waits for them, and re-layouts: 56.9 us -> none  [the longest x65 44.8 us: join_flat(): later[member][:, None, None] * earlier[member + 1] + later[member + 1]]
  transfers between devices with their start and end apart: 4 -> 0, of which waited for: 4 -> 0; matrix products, arithmetic and copies ran while one was open for 17% -> 0% of each run, Pallas kernels for 0% -> 0%
where the time goes in v1:
time: 119 us; the launch traced here: 118 us
  Pallas kernels  105 us (88%)
  local copies, waits for them, and re-layouts  12.6 us (11%)
    pallas_call x1, Pallas kernels, shards(): pl.pallas_call(chain_kernel, out_shape=jax.ShapeDtypeStruct((2, 2, N, WID...  62.7 us
    pallas_call x1, Pallas kernels, shards(): pl.pallas_call(total_kernel, out_shape=(line, line, line), in_specs=[vmem...  20.5 us
    pallas_call x1, Pallas kernels, shards(): pl.pallas_call(output_kernel, grid=(STEPS,), out_shape=(half, half, slim,...  16.4 us
    unnamed x31, local copies, waits for them, and re-layouts  12.6 us
    pallas_call x1, Pallas kernels, shards(): pl.pallas_call(summary_kernel, grid=(STEPS,), out_shape=(jax.ShapeDtypeSt...  5.43 us

profile of v1, /device:TPU:1, one launch (start us, length us, event | category | flops | bytes accessed | tf_op | source)
XLA Modules:
  0.0 118.3 jit_solution(7009310108590102731)
XLA Ops:
  0.6 1.0 copy.17
  1.7 0.0 copy-start
  1.7 1.6 %copy-done = bf16[1,512,2048]{2,1,0:T(8,128)(2,1)S(1)} copy-done((bf16[1,512,2048]{2,1,0:T(8,128)(2,1)S(1)}, bf16[1,512,2048]{2,1,0:T(8,128)(2,1)}, u32[]{:S(2)}) %copy-start) | copy-done | bytes 2097176
  3.3 0.0 copy-start.4
  3.3 0.9 copy-done.4
  4.2 0.0 copy-start.6
  4.2 0.9 copy-done.6
  5.2 0.0 copy-start.9
  5.2 0.7 copy-done.9
  5.8 0.0 copy-start.10
  5.8 0.7 copy-done.10
  6.5 0.0 copy-start.11
  6.5 0.7 copy-done.11
  7.2 0.0 copy-start.5
  7.2 0.0 copy-start.7
  7.2 5.4 %summary.1 = (f32[2,2,64,2048]{3,2,1,0:T(8,128)S(1)}, f32[8,2048]{1,0:T(8,128)S(1)}) custom-call(bf16[512,2048]{1,0:T(8,128)(2,1)S(1)} %bitcast.16, bf16[512,2048]{1,0:T(8,128)(2,1)} %bitcast.18, bf16[512,256]{1,0:T(8,128)(2,1)S(1)} %bitcast.22, bf16[512,256]{1,0:T(8,128)(2,1)S(1)} %bitcast.24, f32[512,64]{1,0:T(8,128)S(1)} %bitcast.20, ...), custom_call_target="tpu_custom_call" | custom-call | flops 1000000000 | bytes 8388608 | tf_op jit(solution)/shard_map/summary/pallas_call | solution.py:414
  12.6 0.0 copy-start.1
  12.6 0.0 copy-start.2
  12.6 0.0 copy-start.12
  12.6 62.7 %chain.1.state_ref = f32[2,2,64,2048]{3,2,1,0:T(8,128)S(1)} custom-call(f32[2,2,64,2048]{3,2,1,0:T(8,128)S(1)} %get-tuple-element.19.part, f32[8,2048]{1,0:T(8,128)S(1)} %get-tuple-element.20.decay), custom_call_target="tpu_custom_call" | custom-call | tf_op jit(solution)/shard_map/chain/pallas_call | solution.py:434
  75.3 0.0 copy-start.3
  75.4 1.3 %copy-done.3 = f32[2,2,64,2048]{3,2,1,0:T(8,128)} copy-done((f32[2,2,64,2048]{3,2,1,0:T(8,128)}, f32[2,2,64,2048]{3,2,1,0:T(8,128)S(1)}, u32[]{:S(2)}) %copy-start.3) | copy-done | bytes 2097176
  76.7 0.0 copy-done.5
  76.7 0.0 copy-done.7
  76.7 0.0 copy-done.1
  76.7 0.0 copy-done.2
  76.7 0.0 copy-done.12
  76.7 16.4 %outputs.1 = (bf16[512,2048]{1,0:T(8,128)(2,1)}, bf16[512,2048]{1,0:T(8,128)(2,1)}, bf16[512,256]{1,0:T(8,128)(2,1)}, bf16[512,256]{1,0:T(8,128)(2,1)}, f32[512,64]{1,0:T(8,128)S(1)}, /*index=5*/f32[8,64]{1,0:T(8,128)S(1)}) custom-call(bf16[512,2048]{1,0:T(8,128)(2,1)S(1)} %bitcast.17, bf16[512,2048]{1,0:T(8,128)(2,1)S(1)} %bitcast.19, ...), custom_call_target="tpu_custom_call" | custom-call | flops 4000000000 | bytes 12582912 | tf_op jit(solution)/shard_map/outputs/pallas_call | solution.py:464
  93.1 0.0 copy-start.8
  93.1 0.6 copy-done.8
  93.7 20.5 %totals.1 = (f32[1,64]{1,0:T(1,128)}, f32[1,64]{1,0:T(1,128)}, f32[1,64]{1,0:T(1,128)}) custom-call(f32[8,64]{1,0:T(8,128)} %copy-done.8), custom_call_target="tpu_custom_call" | custom-call | tf_op jit(solution)/shard_map/totals/pallas_call | solution.py:489
  114.2 0.8 copy.18
  114.9 1.2 copy.22
  116.1 1.1 copy.23
  117.2 1.1 copy.24
Async XLA Ops:
  1.7 1.6 %copy-start = (bf16[1,512,2048]{2,1,0:T(8,128)(2,1)S(1)}, bf16[1,512,2048]{2,1,0:T(8,128)(2,1)}, u32[]{:S(2)}) copy-start(bf16[1,512,2048]{2,1,0:T(8,128)(2,1)} %param.9) | copy-start | bytes 6291460
  3.3 0.9 copy-start.4
  4.2 0.9 copy-start.6
  5.2 0.7 copy-start.9
  5.8 0.7 copy-start.10
  6.5 0.7 copy-start.11
  7.2 69.5 %copy-start.5 = (bf16[1,512,256]{2,1,0:T(8,128)(2,1)S(1)}, bf16[1,512,256]{2,1,0:T(8,128)(2,1)}, u32[]{:S(2)}) copy-start(bf16[1,512,256]{2,1,0:T(8,128)(2,1)} %param.10) | copy-start | bytes 786436
  7.2 69.5 %copy-start.7 = (bf16[1,512,256]{2,1,0:T(8,128)(2,1)S(1)}, bf16[1,512,256]{2,1,0:T(8,128)(2,1)}, u32[]{:S(2)}) copy-start(bf16[1,512,256]{2,1,0:T(8,128)(2,1)} %param.11) | copy-start | bytes 786436
  12.6 64.1 %copy-start.1 = (bf16[1,512,2048]{2,1,0:T(8,128)(2,1)S(1)}, bf16[1,512,2048]{2,1,0:T(8,128)(2,1)}, u32[]{:S(2)}) copy-start(bf16[1,512,2048]{2,1,0:T(8,128)(2,1)} %param.9) | copy-start | bytes 6291460
  12.6 64.1 %copy-start.2 = (bf16[1,512,2048]{2,1,0:T(8,128)(2,1)S(1)}, bf16[1,512,2048]{2,1,0:T(8,128)(2,1)}, u32[]{:S(2)}) copy-start(bf16[1,512,2048]{2,1,0:T(8,128)(2,1)} %param.17) | copy-start | bytes 6291460
  12.6 64.1 %copy-start.12 = (f32[64]{0:T(128)S(1)}, f32[64]{0:T(128)}, u32[]{:S(2)}) copy-start(f32[64]{0:T(128)} %param.15) | copy-start | bytes 772
  75.3 1.3 %copy-start.3 = (f32[2,2,64,2048]{3,2,1,0:T(8,128)}, f32[2,2,64,2048]{3,2,1,0:T(8,128)S(1)}, u32[]{:S(2)}) copy-start(f32[2,2,64,2048]{3,2,1,0:T(8,128)S(1)} %chain.1.state_ref) | copy-start | bytes 6291460
  93.1 0.6 copy-start.8

commit v2 on v0

v2 whole, which is shorter than its diff:
```python
import jax
import jax.numpy as jnp
from jax import lax
from jax.experimental import pallas as pl
from jax.experimental.pallas import tpu as pltpu
from jax.sharding import PartitionSpec as P

H = 64
P_SIZE = 32
N = 64
G = 4
STRETCH = 256
ROWS = 2 * STRETCH
WIDTH = H * P_SIZE
GROUP = WIDTH // G
XY = 16
LANES = 128
TILES = GROUP // LANES
BAND = N // (XY // TILES)
FAR = 8
F32 = jnp.float32
BF16 = jnp.bfloat16
MESH = pl.DeviceIdType.MESH
NN = ((1,), (0,))
NT = ((1,), (1,))
TN = ((0,), (0,))


def dot(a, b, dims=NN, precision=None):
    return lax.dot_general(a, b, (dims, ((), ())), preferred_element_type=F32, precision=precision)


def split(a):
    high = a.astype(BF16)
    return high, (a - high.astype(F32)).astype(BF16)


def triangle(lower):
    row = lax.broadcasted_iota(jnp.int32, (STRETCH, STRETCH), 0)
    column = lax.broadcasted_iota(jnp.int32, (STRETCH, STRETCH), 1)
    return jnp.where(row >= column if lower else row <= column, 1.0, 0.0)


def counts(start_row):
    start = jnp.broadcast_to(start_row.astype(F32), (8, STRETCH)).astype(BF16)
    low = triangle(True).astype(BF16)
    return dot(low, start, NT)[:, :1], dot(start, low, NT)[:1]


def layer_kernel(
    x_hbm, go_hbm, b_hbm, c_hbm, dt_hbm, start_hbm, al_hbm, sk_hbm, tb_hbm,
    mixed, gx, gb, gc, gdt, grad_a, grad_k, grad_t,
    x_v, go_v, b_v, c_v, dt_v, start_v, al, sk, tb,
    heads, dt_s, slope_s, cum_s, u_s, v_s, enter_s, stay_s, seen_s, seen_t,
    y_s, z_s, gb_s, gc_s, net_s, late_s, end_s, skip_s,
    decay, z_decay, part, state, z_in, z_out, up, up_in, down, down_in, params, buf1, buf2,
    in_sem, z_s_sem, z_r_sem, up_s_sem, up_r_sem, down_s_sem, down_r_sem, back_s_sem, back_r_sem,
    s1, r1, s2, r2,
):
    here, dp = lax.axis_index("ctx"), lax.axis_index("dp")
    side, place = lax.rem(here, 2), here // 2
    partner = {"ctx": here + 1 - 2 * side}
    mine_far = dp * 2 + side

    def peer(k):
        return lax.rem(place + k, XY)

    def near(k):
        return {"ctx": peer(k) * 2 + side}

    def far(k):
        g = lax.rem(mine_far + k, FAR)
        return {"dp": g // 2, "ctx": place * 2 + lax.rem(g, 2)}

    loads = []

    def load(src, dst):
        copy = pltpu.make_async_copy(src, dst, in_sem.at[len(loads)])
        copy.start()
        loads.append(copy)
        return copy

    def columns(g):
        return pl.ds(g * GROUP, GROUP)

    small = [load(s, d) for s, d in ((dt_hbm, dt_v), (start_hbm, start_v), (al_hbm, al), (tb_hbm, tb), (sk_hbm, sk))]
    narrow_in = [load(b_hbm, b_v), load(c_hbm, c_v)]
    wide_in = [
        [load(x_hbm.at[:, columns(g)], x_v.at[:, columns(g)]), load(go_hbm.at[:, columns(g)], go_v.at[:, columns(g)])]
        for g in range(G)
    ]

    barrier = pltpu.get_barrier_semaphore()

    def greet_near(k, carry):
        pl.semaphore_signal(barrier, inc=1, device_id=near(k), device_id_type=MESH)
        return carry

    def greet_far(k, carry):
        pl.semaphore_signal(barrier, inc=1, device_id=far(k), device_id_type=MESH)
        return carry

    lax.fori_loop(1, XY, greet_near, 0)
    lax.fori_loop(1, FAR, greet_far, 0)

    def remote(src, dst, send, recv, to):
        return pltpu.make_async_remote_copy(
            src_ref=src, dst_ref=dst, send_sem=send, recv_sem=recv, device_id=to, device_id_type=MESH
        )

    def z_up(g):
        return remote(part.at[1 - side, g], z_in.at[g], z_s_sem.at[g], z_r_sem.at[g], partner)

    def z_decays():
        return remote(decay, z_decay, z_s_sem.at[G], z_r_sem.at[G], partner)

    def up_rows(g):
        return pl.ds(8 + g * 2 * BAND, 2 * BAND) if g else pl.ds(0, 8 + 2 * BAND)

    def up_copy(g, k):
        return remote(up.at[peer(k), up_rows(g)], up_in.at[place, up_rows(g)], up_s_sem.at[g, k], up_r_sem.at[g, k], near(k))

    def down_rows(g):
        return pl.ds(g * 2 * BAND, 2 * BAND)

    def down_copy(g, k):
        return remote(down.at[peer(k), down_rows(g)], down_in.at[place, down_rows(g)], down_s_sem.at[g, k], down_r_sem.at[g, k], near(k))

    def z_back(g):
        return remote(z_out.at[g], state.at[side, g], back_s_sem.at[g], back_r_sem.at[g], partner)

    def each_peer(act):
        def body(k, carry):
            act(k)
            return carry

        lax.fori_loop(1, XY, body, 0)

    head = lax.broadcasted_iota(jnp.int32, (H, WIDTH), 0)
    column = lax.broadcasted_iota(jnp.int32, (H, WIDTH), 1)
    mapped = jnp.where(column // P_SIZE == head, 1.0, 0.0).astype(BF16)
    heads[:H] = mapped
    heads[H:] = mapped
    for copy in small:
        copy.wait()
    rate = -jnp.exp(al[...])
    lows = triangle(True)
    lasts = []
    for block in range(2):
        rows = pl.ds(block * STRETCH, STRETCH)
        shifted = jnp.transpose(dt_v[:, block * STRETCH : (block + 1) * STRETCH]) + tb[...]
        tail = jnp.exp(-jnp.abs(shifted))
        dt = jnp.maximum(shifted, 0.0) + jnp.log1p(tail)
        dt_s[rows] = dt
        slope_s[rows] = jnp.where(shifted >= 0.0, 1.0, tail) / (1.0 + tail)
        cum = rate * dot(lows, dt, precision=lax.Precision.HIGHEST)
        cum_s[rows] = cum
        u_s[rows] = jnp.concatenate(split(jnp.exp(cum)), axis=1)
        v_s[rows] = jnp.concatenate(split(jnp.exp(-cum) * dt), axis=1)
        count, count_row = counts(start_v[:, block * STRETCH : (block + 1) * STRETCH])
        enters = jnp.broadcast_to(jnp.where(count == 0.0, 1.0, 0.0), (STRETCH, N))
        enter_s[rows] = enters
        stay_s[rows] = jnp.broadcast_to(jnp.where(count == count[STRETCH - 1 :], 1.0, 0.0), (STRETCH, N))
        same = jnp.where(count == count_row, 1.0, 0.0)
        seen_s[rows] = same * lows
        seen_t[rows] = same * triangle(False)
        total = dot(u_s[pl.ds((block + 1) * STRETCH - 16, 16)], heads[...])[15:]
        lasts.append(total * jnp.where(count[STRETCH - 1 :] == 0.0, 1.0, 0.0))
    row = lax.broadcasted_iota(jnp.int32, (8, WIDTH), 0)
    decay[...] = jnp.where(row == 0, lasts[0], jnp.where(row == 1, lasts[1], 0.0))
    net_s[...] = jnp.zeros_like(net_s)
    late_s[...] = jnp.zeros_like(late_s)
    end_s[...] = jnp.zeros_like(end_s)
    skip_s[...] = jnp.zeros_like(skip_s)
    skip_row = dot(jnp.concatenate(split(jnp.broadcast_to(sk[...], (8, H))), axis=1), heads[...])[:1]

    def narrow(g):
        return slice(g * N, (g + 1) * N)

    def by_head(values, where):
        high, low = split(values)
        return dot(high, where, NT) + dot(low, where, NT)

    def twice(a, axis):
        return jnp.concatenate([a, a], axis=axis)

    def views(g, block):
        rows, cols = pl.ds(block * STRETCH, STRETCH), columns(g)
        u = dot(u_s[rows], heads[:, cols])
        v = dot(v_s[rows], heads[:, cols])
        x = x_v[rows, cols].astype(F32)
        go = go_v[rows, cols].astype(F32)
        return rows, cols, u, v, x, go

    def kept_rows(ref, mask, g, rows):
        return (ref[rows, narrow(g)].astype(F32) * mask[rows]).astype(BF16)

    def local(g):
        for copy in wide_in[g]:
            copy.wait()
        for block in range(2):
            rows, cols, u, v, x, go = views(g, block)
            xk = jnp.concatenate(split(x * (v * u[STRETCH - 1 :])), axis=0)
            gu = jnp.concatenate(split(go * u), axis=0)
            part[0, g, block] = dot(twice(kept_rows(b_v, stay_s, g, rows), 0), xk, TN)
            part[1, g, 1 - block] = dot(twice(kept_rows(c_v, enter_s, g, rows), 0), gu, TN)

    def intra(g):
        for block in range(2):
            rows, cols, u, v, x, go = views(g, block)
            b_in, c_in = b_v[rows, narrow(g)], c_v[rows, narrow(g)]
            gu, gu_low = split(go * u)
            xv, xv_low = split(x * v)
            scores, scores_low = split(dot(c_in, b_in, NT) * seen_s[rows])
            back, back_low = split(dot(b_in, c_in, NT) * seen_t[rows])
            y_s[rows, cols] = dot(scores, xv) + dot(scores, xv_low) + dot(scores_low, xv)
            z_s[rows, cols] = dot(back, gu) + dot(back, gu_low) + dot(back_low, gu)
            grad_scores = jnp.where(seen_s[rows] > 0.0, dot(gu, xv, NT), 0.0).astype(BF16)
            gc_s[rows, narrow(g)] = dot(grad_scores, b_in)
            gb_s[rows, narrow(g)] = dot(grad_scores, c_in, TN)
            skips = jnp.sum(x * go, axis=0, keepdims=True)
            skip_s[...] += by_head(jnp.broadcast_to(skips, (8, GROUP)), heads[:H, cols])

    def final_sums(g):
        for block in range(2):
            rows, cols, u, v, x, go = views(g, block)
            where = heads[:H, cols]
            entering, later = state[0, g, block], state[1, g, 1 - block]
            c_enter = twice(kept_rows(c_v, enter_s, g, rows), 1)
            b_stay = twice(kept_rows(b_v, stay_s, g, rows), 1)
            y = y_s[rows, cols] + dot(c_enter, jnp.concatenate(split(entering), axis=0))
            from_later = u[STRETCH - 1 :] * dot(b_stay, jnp.concatenate(split(later), axis=0))
            z = z_s[rows, cols] + from_later
            y_s[rows, cols] = y
            z_s[rows, cols] = z
            xv = x * v
            from_z = xv * z
            net_s[rows] += by_head(go * u * y - from_z, where)
            late_s[rows] += by_head(from_z, where)
            ends = jnp.sum(xv * from_later, axis=0, keepdims=True)
            ends += decay[block : block + 1, cols] * jnp.sum(entering * later, axis=0, keepdims=True)
            end_s[block * 8 : (block + 1) * 8] += by_head(jnp.broadcast_to(ends, (8, GROUP)), where)

    def final_out(g):
        skip = skip_row[:, g * GROUP : (g + 1) * GROUP]
        for block in range(2):
            rows, cols, u, v, x, go = views(g, block)
            mixed[rows, cols] = (u * y_s[rows, cols] + skip * x).astype(BF16)
            gx[rows, cols] = (v * z_s[rows, cols] + skip * go).astype(BF16)
            gu = (go * u).astype(BF16)
            xk = (x * (v * u[STRETCH - 1 :])).astype(BF16)
            entering, later = state[0, g, block].astype(BF16), state[1, g, 1 - block].astype(BF16)
            gc[rows, narrow(g)] = (gc_s[rows, narrow(g)] + enter_s[rows] * dot(gu, entering, NT)).astype(BF16)
            gb[rows, narrow(g)] = (gb_s[rows, narrow(g)] + stay_s[rows] * dot(xk, later, NT)).astype(BF16)

    at_zero = side == 0
    first = [at_zero, jnp.logical_not(at_zero)]

    def factors():
        mine = [jnp.where(at_zero, decay[s : s + 1], decay[1 - s : 2 - s]) for s in range(2)]
        theirs = [jnp.where(at_zero, z_decay[s : s + 1], z_decay[1 - s : 2 - s]) for s in range(2)]
        return mine, theirs

    def part_of(row, g):
        return row[:, g * GROUP : (g + 1) * GROUP]

    def combine(g):
        if g == 0:
            z_decays().wait_recv()
        z_up(g).wait_recv()
        mine, theirs = factors()
        if g == 0:
            pair = [mine[s] * theirs[s] for s in range(2)]
            for t in range(TILES):
                lines = [
                    pair[s][:, h * GROUP + t * LANES : h * GROUP + (t + 1) * LANES] for h in range(G) for s in range(2)
                ]
                lines = jnp.concatenate(lines, axis=0)
                for o in range(t, XY, TILES):
                    up[o, :8] = lines
        for s in range(2):
            scale_mine = jnp.where(first[s], part_of(theirs[s], g), 1.0)
            scale_theirs = jnp.where(first[s], 1.0, part_of(mine[s], g))
            total = scale_mine * part[side, g, s] + scale_theirs * z_in[g, s]
            for o in range(XY):
                band, t = o // TILES, o % TILES
                up[o, pl.ds(8 + (2 * g + s) * BAND, BAND)] = total[
                    band * BAND : (band + 1) * BAND, t * LANES : (t + 1) * LANES
                ]
        each_peer(lambda k: up_copy(g, k).start())
        up_in[place, up_rows(g)] = up[place, up_rows(g)]

    def scan(g):
        each_peer(lambda k: up_copy(g, k).wait_recv())

        def rise(j, now):
            down[j, pl.ds(2 * g * BAND, BAND)] = now
            return up_in[j, 2 * g : 2 * g + 1] * now + up_in[j, pl.ds(8 + 2 * g * BAND, BAND)]

        def fall(k, now):
            j = XY - 1 - k
            down[j, pl.ds((2 * g + 1) * BAND, BAND)] = now
            return up_in[j, 2 * g + 1 : 2 * g + 2] * now + up_in[j, pl.ds(8 + (2 * g + 1) * BAND, BAND)]

        now = lax.fori_loop(0, XY, rise, jnp.zeros((BAND, LANES), F32))
        lax.fori_loop(0, XY, fall, now)
        each_peer(lambda k: down_copy(g, k).start())
        down_in[place, down_rows(g)] = down[place, down_rows(g)]

    def spread(g):
        each_peer(lambda k: down_copy(g, k).wait_recv())
        mine, theirs = factors()
        for s in range(2):
            at = pl.ds((2 * g + s) * BAND, BAND)
            enter = jnp.concatenate(
                [
                    jnp.concatenate([down_in[r * TILES + t, at] for t in range(TILES)], axis=1)
                    for r in range(XY // TILES)
                ],
                axis=0,
            )
            keep = jnp.where(first[s], 1.0, part_of(theirs[s], g))
            keep_add = jnp.where(first[s], 0.0, 1.0)
            give = jnp.where(first[s], part_of(mine[s], g), 1.0)
            give_add = jnp.where(first[s], 1.0, 0.0)
            z_out[g, s] = give * enter + give_add * part[side, g, s]
            state[side, g, s] = keep * enter + keep_add * z_in[g, s]
        z_back(g).start()

    for copy in narrow_in:
        copy.wait()
    for g in range(G):
        local(g)
        if g == 0:
            pl.semaphore_wait(barrier, XY + FAR - 2)
            z_decays().start()
        z_up(g).start()
    for g in range(G):
        intra(g)
        combine(g)
        if g >= 1:
            scan(g - 1)
        if g >= 2:
            spread(g - 2)
    scan(G - 1)
    spread(G - 2)
    z_back(0).wait_recv()
    final_sums(0)
    spread(G - 1)
    final_out(0)
    for g in range(1, G):
        z_back(g).wait_recv()
        final_sums(g)
        if g < G - 1:
            final_out(g)

    sum_a = jnp.zeros((1, H), F32)
    sum_t = jnp.zeros((1, H), F32)
    position = lax.broadcasted_iota(jnp.int32, (STRETCH, H), 0)
    for block in range(2):
        rows = pl.ds(block * STRETCH, STRETCH)
        grad_cum = net_s[rows] + jnp.where(position == STRETCH - 1, end_s[block * 8 : block * 8 + 1], 0.0)
        after = dot(triangle(False), grad_cum, precision=lax.Precision.HIGHEST)
        grad_dt = (late_s[rows] / dt_s[rows] + rate * after) * slope_s[rows]
        gdt[:, block * STRETCH : (block + 1) * STRETCH] = jnp.transpose(grad_dt)
        sum_a += jnp.sum(cum_s[rows] * grad_cum, axis=0, keepdims=True)
        sum_t += jnp.sum(grad_dt, axis=0, keepdims=True)
    row = lax.broadcasted_iota(jnp.int32, (8, H), 0)
    params[...] = jnp.where(row == 0, sum_a, jnp.where(row == 1, skip_s[:1], jnp.where(row == 2, sum_t, 0.0)))

    def sum1(k):
        return remote(params, buf1.at[k], s1.at[k], r1.at[k], near(k))

    def sum2(k):
        return remote(buf2.at[0], buf2.at[k], s2.at[k], r2.at[k], far(k))

    def each_far(act):
        def body(k, carry):
            act(k)
            return carry

        lax.fori_loop(1, FAR, body, 0)

    each_peer(lambda k: sum1(k).start())
    buf1[0] = params[...]
    final_out(G - 1)
    for g in range(G):
        z_back(g).wait_send()
        z_up(g).wait_send()
        each_peer(lambda k: up_copy(g, k).wait_send())
        each_peer(lambda k: down_copy(g, k).wait_send())
    z_decays().wait_send()
    each_peer(lambda k: sum1(k).wait_recv())
    buf2[0] = jnp.sum(buf1[...], axis=0)
    each_far(lambda k: sum2(k).start())
    each_peer(lambda k: sum1(k).wait_send())
    each_far(lambda k: sum2(k).wait_recv())
    total = jnp.zeros((8, H), F32)
    for g in range(FAR):
        total += buf2[lax.rem(g - mine_far + FAR, FAR)]
    grad_a[...] = total[0:1]
    grad_k[...] = total[1:2]
    grad_t[...] = total[2:3]
    each_far(lambda k: sum2(k).wait_send())


def store_kernel(*refs):
    count = len(refs) // 2
    sems = refs[-1]
    copies = [pltpu.make_async_copy(refs[i], refs[count + i], sems.at[i]) for i in range(count)]
    for copy in copies:
        copy.start()
    for copy in copies:
        copy.wait()


def shards(hidden_x, b_proj, c_proj, dt_raw, span_start, a_log, skip_gain, dt_bias, out_grad):
    arrays = (
        hidden_x.reshape(ROWS, WIDTH),
        out_grad.reshape(ROWS, WIDTH),
        b_proj.reshape(ROWS, G * N),
        c_proj.reshape(ROWS, G * N),
        dt_raw.reshape(ROWS, H).T,
        span_start.reshape(1, ROWS),
        a_log.reshape(1, H),
        skip_gain.reshape(1, H),
        dt_bias.reshape(1, H),
    )
    anywhere = pl.BlockSpec(memory_space=pltpu.HBM)
    vmem = pl.BlockSpec(memory_space=pltpu.VMEM)
    dma = pltpu.SemaphoreType.DMA

    def f32(*shape):
        return pltpu.VMEM(shape, F32)

    def bf16(*shape):
        return pltpu.VMEM(shape, BF16)

    wide = jax.ShapeDtypeStruct((ROWS, WIDTH), BF16)
    slim = jax.ShapeDtypeStruct((ROWS, G * N), BF16)
    line = jax.ShapeDtypeStruct((1, H), F32)
    outs = (wide, wide, slim, slim, jax.ShapeDtypeStruct((H, ROWS), F32), line, line, line)
    held = tuple(pltpu.VMEM(out.shape, out.dtype) for out in outs)
    arrays = [pltpu.with_memory_space_constraint(a, pltpu.HBM) for a in arrays]
    results = pl.pallas_call(
        layer_kernel,
        out_shape=held,
        in_specs=[anywhere] * len(arrays),
        out_specs=(vmem,) * len(outs),
        scratch_shapes=[
            bf16(ROWS, WIDTH), bf16(ROWS, WIDTH), bf16(ROWS, G * N), bf16(ROWS, G * N), f32(H, ROWS),
            pltpu.VMEM((1, ROWS), jnp.int32), f32(1, H), f32(1, H), f32(1, H),
            bf16(2 * H, WIDTH), f32(ROWS, H), f32(ROWS, H), f32(ROWS, H), bf16(ROWS, 2 * H), bf16(ROWS, 2 * H),
            f32(ROWS, N), f32(ROWS, N), f32(ROWS, STRETCH), f32(ROWS, STRETCH),
            f32(ROWS, WIDTH), f32(ROWS, WIDTH),
            f32(ROWS, G * N), f32(ROWS, G * N), f32(ROWS, H), f32(ROWS, H), f32(16, H), f32(8, H),
            f32(8, WIDTH), f32(8, WIDTH),
            f32(2, G, 2, N, GROUP), f32(2, G, 2, N, GROUP), f32(G, 2, N, GROUP), f32(G, 2, N, GROUP),
            f32(XY, 8 + 2 * N, LANES), f32(XY, 8 + 2 * N, LANES), f32(XY, 2 * N, LANES), f32(XY, 2 * N, LANES),
            f32(8, H), f32(XY, 8, H), f32(FAR, 8, H),
            dma((7 + 2 * G,)), dma((G + 1,)), dma((G + 1,)),
            dma((G, XY)), dma((G, XY)), dma((G, XY)), dma((G, XY)), dma((G,)), dma((G,)),
            dma((XY,)), dma((XY,)), dma((FAR,)), dma((FAR,)),
        ],
        compiler_params=pltpu.CompilerParams(
            collective_id=0, has_side_effects=True, vmem_limit_bytes=44 * 2**20
        ),
        cost_estimate=pl.CostEstimate(flops=5 * 10**9, bytes_accessed=10 * 2**20, transcendentals=10**5),
        name="layer",
    )(*arrays)
    mixed, gx, gb, gc, gdt, grad_a, grad_k, grad_t = pl.pallas_call(
        store_kernel,
        out_shape=outs,
        in_specs=[vmem] * len(outs),
        out_specs=(anywhere,) * len(outs),
        scratch_shapes=[dma((len(outs),))],
        compiler_params=pltpu.CompilerParams(vmem_limit_bytes=2**20),
        name="store",
    )(*[pltpu.with_memory_space_constraint(r, pltpu.VMEM) for r in results])
    return (
        mixed.reshape(1, ROWS, WIDTH),
        gx.reshape(1, ROWS, WIDTH),
        gb.reshape(1, ROWS, G * N),
        gc.reshape(1, ROWS, G * N),
        gdt.T.reshape(1, ROWS, H),
        grad_a.reshape(H),
        grad_k.reshape(H),
        grad_t.reshape(H),
    )


def solution(mesh):
    rows = P("dp", "ctx", None)
    return jax.shard_map(
        shards,
        mesh=mesh,
        in_specs=(rows, rows, rows, rows, P("dp", "ctx"), P(), P(), P(), rows),
        out_specs=(rows, rows, rows, rows, rows, P(), P(), P()),
        check_vma=False,
    )
```

time: 1450 us -> 74.9 us (0.05); the launches traced: 1430 us -> 74.8 us
  waiting for transfers between devices: 501 us -> 0 us
  blocking collectives: 376 us -> 0 us
  other arithmetic: 317 us -> 0 us
  local copies, waits for them, and re-layouts: 131 us -> 0 us
  matrix products: 87 us -> 0 us
  Pallas kernels: 0 us -> 74 us
  between operations: 15.6 us -> 0.8 us
    all_gather x4 -> x0, waiting for transfers between devices: 501 us -> none  [prefix(): everything = jax.tree.map(lambda part: lax.all_gather(part, axis), array)]
    select_n x198 -> x0, other arithmetic: 281 us -> none  [the longest x192 273 us: lap(): return jax.tree.map(lambda a, b: jnp.where(reached, a, b), new, before)]
    all_gather x2 -> x0, blocking collectives: 158 us -> none  [prefix(): everything = jax.tree.map(lambda part: lax.all_gather(part, axis), array)]
    unnamed x1 -> x0, blocking collectives: 154 us -> none
    dot_general x12 -> x0, matrix products: 87 us -> none  [the longest x3 47.6 us: stretch_output(): jnp.einsum('gkts,sgkp->tgkp', mixing, x_half.reshape(length, G, heads_per...]
    pallas_call x0 -> x2, Pallas kernels: none -> 74 us  [the longest x1 71.7 us: shards(): pl.pallas_call(layer_kernel, out_shape=held, in_specs=[anywhere] * len(ar...]
    psum x1 -> x0, blocking collectives: 64.5 us -> none  [shards(): lax.psum((grad_ao + grad_as, grad_ko, grad_to + grad_ts), ('dp', 'ctx'))]
    mul x69 -> x0, local copies, waits for them, and re-layouts: 56.9 us -> none  [the longest x65 44.8 us: join_flat(): later[member][:, None, None] * earlier[member + 1] + later[member + 1]]
  transfers between devices with their start and end apart: 4 -> 0, of which waited for: 4 -> 0; matrix products, arithmetic and copies ran while one was open for 17% -> 0% of each run, Pallas kernels for 0% -> 0%
where the time goes in v2:
time: 74.9 us; the launch traced here: 74.8 us
  Pallas kernels  74 us (99%)
  between operations  0.8 us (1%)
    pallas_call x1, Pallas kernels, shards(): pl.pallas_call(layer_kernel, out_shape=held, in_specs=[anywhere] * len(ar...  71.7 us
    pallas_call x1, Pallas kernels, shards(): pl.pallas_call(store_kernel, out_shape=outs, in_specs=[vmem] * len(outs),...  2.27 us

profile of v2, /device:TPU:1, one launch (start us, length us, event | category | flops | bytes accessed | tf_op | source)
XLA Modules:
  0.0 74.8 jit_solution(13123464885936665754)
XLA Ops:
  0.6 71.7 %layer.1 = (bf16[512,2048]{1,0:T(8,128)(2,1)S(1)}, bf16[512,2048]{1,0:T(8,128)(2,1)S(1)}, bf16[512,256]{1,0:T(8,128)(2,1)S(1)}, bf16[512,256]{1,0:T(8,128)(2,1)S...) custom-call(bf16[512,2048]{1,0:T(8,128)(2,1)} %bitcast.20, ...), custom_call_target="tpu_custom_call" | custom-call | flops 5000000000 | bytes 10485760 | tf_op jit(solution)/shard_map/layer/pallas_call | solution.py:445
  72.4 2.3 %store.1 = (bf16[512,2048]{1,0:T(8,128)(2,1)}, bf16[512,2048]{1,0:T(8,128)(2,1)}, bf16[512,256]{1,0:T(8,128)(2,1)}, bf16[512,256]{1,0:T(8,128)(2,1)}, f32[64,512...) custom-call(bf16[512,2048]{1,0:T(8,128)(2,1)S(1)} %get-tuple-element.24.refs_0_, ...), custom_call_target="tpu_custom_call" | custom-call | tf_op jit(solution)/shard_map/store/pallas_call | solution.py:471

commit v3 on v2

--- a/solution.py
+++ b/solution.py
@@ -18,6 +18,7 @@
 TILES = GROUP // LANES
 BAND = N // (XY // TILES)
 FAR = 8
+PIECES = 4
 F32 = jnp.float32
 BF16 = jnp.bfloat16
 MESH = pl.DeviceIdType.MESH
@@ -41,19 +42,13 @@
     return jnp.where(row >= column if lower else row <= column, 1.0, 0.0)
 
 
-def counts(start_row):
-    start = jnp.broadcast_to(start_row.astype(F32), (8, STRETCH)).astype(BF16)
-    low = triangle(True).astype(BF16)
-    return dot(low, start, NT)[:, :1], dot(start, low, NT)[:1]
-
-
 def layer_kernel(
     x_hbm, go_hbm, b_hbm, c_hbm, dt_hbm, start_hbm, al_hbm, sk_hbm, tb_hbm,
     mixed, gx, gb, gc, gdt, grad_a, grad_k, grad_t,
-    x_v, go_v, b_v, c_v, dt_v, start_v, al, sk, tb,
-    heads, dt_s, slope_s, cum_s, u_s, v_s, enter_s, stay_s, seen_s, seen_t,
-    y_s, z_s, gb_s, gc_s, net_s, late_s, end_s, skip_s,
-    decay, z_decay, part, state, z_in, z_out, up, up_in, down, down_in, params, buf1, buf2,
+    wide, b_v, c_v, dt_v, start_v, al, sk, tb,
+    heads, dt_s, slope_s, cum_s, factor, v_s, masked, enter_s, stay_s, seen_s, seen_t,
+    y_s, z_s, gb_s, gc_s, net_s, late_s, end_s, skip_s, weigh_s, ahead_s, early_s,
+    ends_here, ends_there, decay, z_decay, part, state, z_in, z_out, up, up_in, down, down_in, params, buf1, buf2,
     in_sem, z_s_sem, z_r_sem, up_s_sem, up_r_sem, down_s_sem, down_r_sem, back_s_sem, back_r_sem,
     s1, r1, s2, r2,
 ):
@@ -86,7 +81,7 @@
     small = [load(s, d) for s, d in ((dt_hbm, dt_v), (start_hbm, start_v), (al_hbm, al), (tb_hbm, tb), (sk_hbm, sk))]
     narrow_in = [load(b_hbm, b_v), load(c_hbm, c_v)]
     wide_in = [
-        [load(x_hbm.at[:, columns(g)], x_v.at[:, columns(g)]), load(go_hbm.at[:, columns(g)], go_v.at[:, columns(g)])]
+        [load(x_hbm.at[:, columns(g)], wide.at[0, :, columns(g)]), load(go_hbm.at[:, columns(g)], wide.at[1, :, columns(g)])]
         for g in range(G)
     ]
 
@@ -112,7 +107,7 @@
         return remote(part.at[1 - side, g], z_in.at[g], z_s_sem.at[g], z_r_sem.at[g], partner)
 
     def z_decays():
-        return remote(decay, z_decay, z_s_sem.at[G], z_r_sem.at[G], partner)
+        return remote(ends_here, ends_there, z_s_sem.at[G], z_r_sem.at[G], partner)
 
     def up_rows(g):
         return pl.ds(8 + g * 2 * BAND, 2 * BAND) if g else pl.ds(0, 8 + 2 * BAND)
@@ -136,16 +131,23 @@
 
         lax.fori_loop(1, XY, body, 0)
 
-    head = lax.broadcasted_iota(jnp.int32, (H, WIDTH), 0)
-    column = lax.broadcasted_iota(jnp.int32, (H, WIDTH), 1)
-    mapped = jnp.where(column // P_SIZE == head, 1.0, 0.0).astype(BF16)
-    heads[:H] = mapped
-    heads[H:] = mapped
-    for copy in small:
+    def map_heads(g):
+        head = lax.broadcasted_iota(jnp.int32, (H, GROUP), 0)
+        column = lax.broadcasted_iota(jnp.int32, (H, GROUP), 1) + g * GROUP
+        mapped = jnp.where(column // P_SIZE == head, 1.0, 0.0).astype(BF16)
+        heads[:H, columns(g)] = mapped
+        heads[H:, columns(g)] = mapped
+
+    def expand(values):
+        return dot(jnp.concatenate(split(values), axis=1), heads[...])
+
+    map_heads(0)
+    lows = triangle(True)
+    lows_half = lows.astype(BF16)
+    for copy in small + narrow_in:
         copy.wait()
     rate = -jnp.exp(al[...])
-    lows = triangle(True)
-    lasts = []
+    lasts, spans = [], []
     for block in range(2):
         rows = pl.ds(block * STRETCH, STRETCH)
         shifted = jnp.transpose(dt_v[:, block * STRETCH : (block + 1) * STRETCH]) + tb[...]
@@ -153,26 +155,42 @@
         dt = jnp.maximum(shifted, 0.0) + jnp.log1p(tail)
         dt_s[rows] = dt
         slope_s[rows] = jnp.where(shifted >= 0.0, 1.0, tail) / (1.0 + tail)
-        cum = rate * dot(lows, dt, precision=lax.Precision.HIGHEST)
+        dt_high, dt_rest = split(dt)
+        dt_low = (dt - dt_high.astype(F32) - dt_rest.astype(F32)).astype(BF16)
+        cum = rate * (dot(lows_half, dt_high) + dot(lows_half, dt_rest) + dot(lows_half, dt_low))
         cum_s[rows] = cum
-        u_s[rows] = jnp.concatenate(split(jnp.exp(cum)), axis=1)
+        last = cum[STRETCH - 1 :]
+        factor[0, rows] = jnp.concatenate(split(jnp.exp(last - cum) * dt), axis=1)
+        factor[1, rows] = jnp.concatenate(split(jnp.exp(cum)), axis=1)
         v_s[rows] = jnp.concatenate(split(jnp.exp(-cum) * dt), axis=1)
-        count, count_row = counts(start_v[:, block * STRETCH : (block + 1) * STRETCH])
-        enters = jnp.broadcast_to(jnp.where(count == 0.0, 1.0, 0.0), (STRETCH, N))
-        enter_s[rows] = enters
-        stay_s[rows] = jnp.broadcast_to(jnp.where(count == count[STRETCH - 1 :], 1.0, 0.0), (STRETCH, N))
-        same = jnp.where(count == count_row, 1.0, 0.0)
-        seen_s[rows] = same * lows
-        seen_t[rows] = same * triangle(False)
-        total = dot(u_s[pl.ds((block + 1) * STRETCH - 16, 16)], heads[...])[15:]
-        lasts.append(total * jnp.where(count[STRETCH - 1 :] == 0.0, 1.0, 0.0))
-    row = lax.broadcasted_iota(jnp.int32, (8, WIDTH), 0)
-    decay[...] = jnp.where(row == 0, lasts[0], jnp.where(row == 1, lasts[1], 0.0))
-    net_s[...] = jnp.zeros_like(net_s)
-    late_s[...] = jnp.zeros_like(late_s)
-    end_s[...] = jnp.zeros_like(end_s)
-    skip_s[...] = jnp.zeros_like(skip_s)
-    skip_row = dot(jnp.concatenate(split(jnp.broadcast_to(sk[...], (8, H))), axis=1), heads[...])[:1]
+        start = jnp.broadcast_to(start_v[:, block * STRETCH : (block + 1) * STRETCH].astype(F32), (8, STRETCH))
+        start = start.astype(BF16)
+        count = dot(lows_half, start, NT)[:, :1]
+        spans.append((count, start))
+        enters = jnp.where(count == 0.0, 1.0, 0.0)
+        stays = jnp.where(count == count[STRETCH - 1 :], 1.0, 0.0)
+        masked[0, rows] = (b_v[rows].astype(F32) * stays).astype(BF16)
+        masked[1, rows] = (c_v[rows].astype(F32) * enters).astype(BF16)
+        enter_s[rows] = jnp.broadcast_to(enters, (STRETCH, N))
+        stay_s[rows] = jnp.broadcast_to(stays, (STRETCH, N))
+        lasts.append(jnp.exp(last) * jnp.where(count[STRETCH - 1 :] == 0.0, 1.0, 0.0))
+    row = lax.broadcasted_iota(jnp.int32, (8, H), 0)
+    ends_here[...] = jnp.where(row == 0, lasts[0], jnp.where(row == 1, lasts[1], 0.0))
+
+    def prepare():
+        for g in range(1, G):
+            map_heads(g)
+        for block in range(2):
+            rows = pl.ds(block * STRETCH, STRETCH)
+            count, start = spans[block]
+            same = jnp.where(count == dot(start, lows_half, NT)[:1], 1.0, 0.0)
+            seen_s[rows] = same * lows
+            seen_t[rows] = same * triangle(False)
+        decay[...] = expand(ends_here[...])
+        net_s[...] = jnp.zeros_like(net_s)
+        late_s[...] = jnp.zeros_like(late_s)
+        end_s[...] = jnp.zeros_like(end_s)
+        skip_s[...] = jnp.zeros_like(skip_s)
 
     def narrow(g):
         return slice(g * N, (g + 1) * N)
@@ -186,24 +204,19 @@
 
     def views(g, block):
         rows, cols = pl.ds(block * STRETCH, STRETCH), columns(g)
-        u = dot(u_s[rows], heads[:, cols])
+        u = dot(factor[1, rows], heads[:, cols])
         v = dot(v_s[rows], heads[:, cols])
-        x = x_v[rows, cols].astype(F32)
-        go = go_v[rows, cols].astype(F32)
+        x = wide[0, rows, cols].astype(F32)
+        go = wide[1, rows, cols].astype(F32)
         return rows, cols, u, v, x, go
 
-    def kept_rows(ref, mask, g, rows):
-        return (ref[rows, narrow(g)].astype(F32) * mask[rows]).astype(BF16)
-
-    def local(g):
-        for copy in wide_in[g]:
-            copy.wait()
-        for block in range(2):
-            rows, cols, u, v, x, go = views(g, block)
-            xk = jnp.concatenate(split(x * (v * u[STRETCH - 1 :])), axis=0)
-            gu = jnp.concatenate(split(go * u), axis=0)
-            part[0, g, block] = dot(twice(kept_rows(b_v, stay_s, g, rows), 0), xk, TN)
-            part[1, g, 1 - block] = dot(twice(kept_rows(c_v, enter_s, g, rows), 0), gu, TN)
+    def local(d, g):
+        cols = columns(g)
+        for block in range(2):
+            rows = pl.ds(block * STRETCH, STRETCH)
+            scaled = wide[d, rows, cols].astype(F32) * dot(factor[d, rows], heads[:, cols])
+            scaled = jnp.concatenate(split(scaled), axis=0)
+            part[d, g, lax.rem(block + d, 2)] = dot(twice(masked[d, rows, narrow(g)], 0), scaled, TN)
 
     def intra(g):
         for block in range(2):
@@ -220,20 +233,81 @@
             gb_s[rows, narrow(g)] = dot(grad_scores, c_in, TN)
             skips = jnp.sum(x * go, axis=0, keepdims=True)
             skip_s[...] += by_head(jnp.broadcast_to(skips, (8, GROUP)), heads[:H, cols])
+            if g == G - 1:
+                from_z = x * v * z_s[rows, cols]
+                net_s[rows] += by_head(go * u * y_s[rows, cols] - from_z, heads[:H, cols])
+                late_s[rows] += by_head(from_z, heads[:H, cols])
+
+    def weigh():
+        g = G - 1
+        cols = columns(g)
+        for block in range(2):
+            rows = pl.ds(block * STRETCH, STRETCH)
+            x = wide[0, rows, cols].astype(F32)
+            go = wide[1, rows, cols].astype(F32)
+            cum, slope, dt = cum_s[rows], slope_s[rows], dt_s[rows]
+            reach = rate * sum(dot(lows_half, part_slope) for part_slope in split(slope))
+            u, k = jnp.exp(cum), jnp.exp(cum[STRETCH - 1 :] - cum) * dt
+            plans = ((cum, -cum), (reach, slope / dt - reach))
+            for kind, (on_states, on_later) in enumerate(plans):
+                ahead = dot(jnp.concatenate(split(u * on_states), axis=1), heads[:, cols]) * go
+                behind = dot(jnp.concatenate(split(k * on_later), axis=1), heads[:, cols]) * x
+                ahead = jnp.concatenate(split(ahead), axis=0)
+                behind = jnp.concatenate(split(behind), axis=0)
+                at_end = jnp.broadcast_to(on_states[STRETCH - 1 :], (8, H))
+                at_end = dot(jnp.concatenate(split(at_end), axis=1), heads[:, cols])
+                weigh_s[kind, block, 0] = dot(twice(masked[1, rows, narrow(g)], 0), ahead, TN)
+                weigh_s[kind, block, 1] = (
+                    dot(twice(masked[0, rows, narrow(g)], 0), behind, TN) + at_end[:1] * part[0, g, block]
+                )
+                ahead_s[kind, block] = at_end * decay[block : block + 1, cols]
+
+    def last_sums():
+        lines = []
+        for kind in range(2):
+            line = jnp.zeros((1, GROUP), F32)
+            for block in range(2):
+                entering, later = state[0, G - 1, block], state[1, G - 1, 1 - block]
+                line += jnp.sum(entering * weigh_s[kind, block, 0] + later * weigh_s[kind, block, 1], axis=0, keepdims=True)
+                line += ahead_s[kind, block, :1] * jnp.sum(entering * later, axis=0, keepdims=True)
+            lines.append(line)
+        row = lax.broadcasted_iota(jnp.int32, (8, GROUP), 0)
+        lines = jnp.where(row == 0, lines[0], jnp.where(row == 1, lines[1], 0.0))
+        return by_head(lines, heads[:H, columns(G - 1)])
+
+    def dt_gradients(block):
+        rows = pl.ds(block * STRETCH, STRETCH)
+        position = lax.broadcasted_iota(jnp.int32, (STRETCH, H), 0)
+        grad_cum = net_s[rows] + jnp.where(position == STRETCH - 1, end_s[block * 8 : block * 8 + 1], 0.0)
+        after = dot(triangle(False), grad_cum, precision=lax.Precision.HIGHEST)
+        return grad_cum, (late_s[rows] / dt_s[rows] + rate * after) * slope_s[rows]
+
+    def early_sums():
+        sum_a = jnp.zeros((1, H), F32)
+        sum_t = jnp.zeros((1, H), F32)
+        for block in range(2):
+            grad_cum, grad_dt = dt_gradients(block)
+            sum_a += jnp.sum(cum_s[pl.ds(block * STRETCH, STRETCH)] * grad_cum, axis=0, keepdims=True)
+            sum_t += jnp.sum(grad_dt, axis=0, keepdims=True)
+        row = lax.broadcasted_iota(jnp.int32, (8, H), 0)
+        early_s[...] = jnp.where(row == 0, sum_a, jnp.where(row == 1, sum_t, jnp.where(row == 2, skip_s[:1], 0.0)))
 
     def final_sums(g):
         for block in range(2):
             rows, cols, u, v, x, go = views(g, block)
             where = heads[:H, cols]
             entering, later = state[0, g, block], state[1, g, 1 - block]
-            c_enter = twice(kept_rows(c_v, enter_s, g, rows), 1)
-            b_stay = twice(kept_rows(b_v, stay_s, g, rows), 1)
-            y = y_s[rows, cols] + dot(c_enter, jnp.concatenate(split(entering), axis=0))
+            c_enter = twice(masked[1, rows, narrow(g)], 1)
+            b_stay = twice(masked[0, rows, narrow(g)], 1)
+            from_state = dot(c_enter, jnp.concatenate(split(entering), axis=0))
+            y = y_s[rows, cols] + from_state
             from_later = u[STRETCH - 1 :] * dot(b_stay, jnp.concatenate(split(later), axis=0))
             z = z_s[rows, cols] + from_later
             y_s[rows, cols] = y
             z_s[rows, cols] = z
             xv = x * v
+            if g == G - 1:
+                y, z = from_state, from_later
             from_z = xv * z
             net_s[rows] += by_head(go * u * y - from_z, where)
             late_s[rows] += by_head(from_z, where)
@@ -267,6 +341,7 @@
     def combine(g):
         if g == 0:
             z_decays().wait_recv()
+            z_decay[...] = expand(ends_there[...])
         z_up(g).wait_recv()
         mine, theirs = factors()
         if g == 0:
@@ -327,14 +402,21 @@
             state[side, g, s] = keep * enter + keep_add * z_in[g, s]
         z_back(g).start()
 
-    for copy in narrow_in:
+    for copy in wide_in[0]:
         copy.wait()
+    local(1 - side, 0)
+    pl.semaphore_wait(barrier, XY + FAR - 2)
+    z_decays().start()
+    z_up(0).start()
+    prepare()
+    skip_row = expand(jnp.broadcast_to(sk[...], (8, H)))[:1]
+    for g in range(1, G):
+        for copy in wide_in[g]:
+            copy.wait()
+        local(1 - side, g)
+        z_up(g).start()
     for g in range(G):
-        local(g)
-        if g == 0:
-            pl.semaphore_wait(barrier, XY + FAR - 2)
-            z_decays().start()
-        z_up(g).start()
+        local(side, g)
     for g in range(G):
         intra(g)
         combine(g)
@@ -348,25 +430,21 @@
     final_sums(0)
     spread(G - 1)
     final_out(0)
-    for g in range(1, G):
+    for g in range(G):
+        z_up(g).wait_send()
+        each_peer(lambda k: up_copy(g, k).wait_send())
+        each_peer(lambda k: down_copy(g, k).wait_send())
+    z_decays().wait_send()
+    weigh()
+    for g in range(1, G - 1):
         z_back(g).wait_recv()
         final_sums(g)
-        if g < G - 1:
-            final_out(g)
-
-    sum_a = jnp.zeros((1, H), F32)
-    sum_t = jnp.zeros((1, H), F32)
-    position = lax.broadcasted_iota(jnp.int32, (STRETCH, H), 0)
-    for block in range(2):
-        rows = pl.ds(block * STRETCH, STRETCH)
-        grad_cum = net_s[rows] + jnp.where(position == STRETCH - 1, end_s[block * 8 : block * 8 + 1], 0.0)
-        after = dot(triangle(False), grad_cum, precision=lax.Precision.HIGHEST)
-        grad_dt = (late_s[rows] / dt_s[rows] + rate * after) * slope_s[rows]
-        gdt[:, block * STRETCH : (block + 1) * STRETCH] = jnp.transpose(grad_dt)
-        sum_a += jnp.sum(cum_s[rows] * grad_cum, axis=0, keepdims=True)
-        sum_t += jnp.sum(grad_dt, axis=0, keepdims=True)
-    row = lax.broadcasted_iota(jnp.int32, (8, H), 0)
-    params[...] = jnp.where(row == 0, sum_a, jnp.where(row == 1, skip_s[:1], jnp.where(row == 2, sum_t, 0.0)))
+        final_out(g)
+    early_sums()
+    for g in range(G):
+        z_back(g).wait_send()
+    z_back(G - 1).wait_recv()
+    params[...] = early_s[...] + last_sums()
 
     def sum1(k):
         return remote(params, buf1.at[k], s1.at[k], r1.at[k], near(k))
@@ -383,13 +461,10 @@
 
     each_peer(lambda k: sum1(k).start())
     buf1[0] = params[...]
+    final_sums(G - 1)
     final_out(G - 1)
-    for g in range(G):
-        z_back(g).wait_send()
-        z_up(g).wait_send()
-        each_peer(lambda k: up_copy(g, k).wait_send())
-        each_peer(lambda k: down_copy(g, k).wait_send())
-    z_decays().wait_send()
+    for block in range(2):
+        gdt[:, block * STRETCH : (block + 1) * STRETCH] = jnp.transpose(dt_gradients(block)[1])
     each_peer(lambda k: sum1(k).wait_recv())
     buf2[0] = jnp.sum(buf1[...], axis=0)
     each_far(lambda k: sum2(k).start())
@@ -399,17 +474,22 @@
     for g in range(FAR):
         total += buf2[lax.rem(g - mine_far + FAR, FAR)]
     grad_a[...] = total[0:1]
-    grad_k[...] = total[1:2]
-    grad_t[...] = total[2:3]
+    grad_t[...] = total[1:2]
+    grad_k[...] = total[2:3]
     each_far(lambda k: sum2(k).wait_send())
 
 
 def store_kernel(*refs):
     count = len(refs) // 2
     sems = refs[-1]
-    copies = [pltpu.make_async_copy(refs[i], refs[count + i], sems.at[i]) for i in range(count)]
-    for copy in copies:
-        copy.start()
+    copies = []
+    for src, dst in zip(refs[:count], refs[count:]):
+        pieces = PIECES if src.shape[0] == ROWS else 1
+        for i in range(pieces):
+            rows = pl.ds(i * (src.shape[0] // pieces), src.shape[0] // pieces)
+            copy = pltpu.make_async_copy(src.at[rows], dst.at[rows], sems.at[len(copies)])
+            copy.start()
+            copies.append(copy)
     for copy in copies:
         copy.wait()
 
@@ -448,13 +528,14 @@
         in_specs=[anywhere] * len(arrays),
         out_specs=(vmem,) * len(outs),
         scratch_shapes=[
-            bf16(ROWS, WIDTH), bf16(ROWS, WIDTH), bf16(ROWS, G * N), bf16(ROWS, G * N), f32(H, ROWS),
+            bf16(2, ROWS, WIDTH), bf16(ROWS, G * N), bf16(ROWS, G * N), f32(H, ROWS),
             pltpu.VMEM((1, ROWS), jnp.int32), f32(1, H), f32(1, H), f32(1, H),
-            bf16(2 * H, WIDTH), f32(ROWS, H), f32(ROWS, H), f32(ROWS, H), bf16(ROWS, 2 * H), bf16(ROWS, 2 * H),
-            f32(ROWS, N), f32(ROWS, N), f32(ROWS, STRETCH), f32(ROWS, STRETCH),
+            bf16(2 * H, WIDTH), f32(ROWS, H), f32(ROWS, H), f32(ROWS, H), bf16(2, ROWS, 2 * H), bf16(ROWS, 2 * H),
+            bf16(2, ROWS, G * N), f32(ROWS, N), f32(ROWS, N), f32(ROWS, STRETCH), f32(ROWS, STRETCH),
             f32(ROWS, WIDTH), f32(ROWS, WIDTH),
             f32(ROWS, G * N), f32(ROWS, G * N), f32(ROWS, H), f32(ROWS, H), f32(16, H), f32(8, H),
-            f32(8, WIDTH), f32(8, WIDTH),
+            f32(2, 2, 2, N, GROUP), f32(2, 2, 8, GROUP), f32(8, H),
+            f32(8, H), f32(8, H), f32(8, WIDTH), f32(8, WIDTH),
             f32(2, G, 2, N, GROUP), f32(2, G, 2, N, GROUP), f32(G, 2, N, GROUP), f32(G, 2, N, GROUP),
             f32(XY, 8 + 2 * N, LANES), f32(XY, 8 + 2 * N, LANES), f32(XY, 2 * N, LANES), f32(XY, 2 * N, LANES),
             f32(8, H), f32(XY, 8, H), f32(FAR, 8, H),
@@ -473,7 +554,7 @@
         out_shape=outs,
         in_specs=[vmem] * len(outs),
         out_specs=(anywhere,) * len(outs),
-        scratch_shapes=[dma((len(outs),))],
+        scratch_shapes=[dma((4 * PIECES + 4,))],
         compiler_params=pltpu.CompilerParams(vmem_limit_bytes=2**20),
         name="store",
     )(*[pltpu.with_memory_space_constraint(r, pltpu.VMEM) for r in results])

time: 74.9 us -> 71.7 us (0.957)
  Pallas kernels: 74 us -> 70.7 us
    pallas_call x1, Pallas kernels: 71.7 us -> 68.4 us  [shards(): pl.pallas_call(layer_kernel, out_shape=held, in_specs=[anywhere] * len(ar...]
where the time goes in v3:
time: 71.7 us; the launch traced here: 71.5 us
  Pallas kernels  70.7 us (99%)
  between operations  0.8 us (1%)
    pallas_call x1, Pallas kernels, shards(): pl.pallas_call(layer_kernel, out_shape=held, in_specs=[anywhere] * len(ar...  68.4 us
    pallas_call x1, Pallas kernels, shards(): pl.pallas_call(store_kernel, out_shape=outs, in_specs=[vmem] * len(outs),...  2.38 us

profile of v3, /device:TPU:1, one launch (start us, length us, event | category | flops | bytes accessed | tf_op | source)
XLA Modules:
  0.0 71.5 jit_solution(8750105952660992301)
XLA Ops:
  0.6 68.4 %layer.1 = (bf16[512,2048]{1,0:T(8,128)(2,1)S(1)}, bf16[512,2048]{1,0:T(8,128)(2,1)S(1)}, bf16[512,256]{1,0:T(8,128)(2,1)S(1)}, bf16[512,256]{1,0:T(8,128)(2,1)S...) custom-call(bf16[512,2048]{1,0:T(8,128)(2,1)} %bitcast.20, ...), custom_call_target="tpu_custom_call" | custom-call | flops 5000000000 | bytes 10485760 | tf_op jit(solution)/shard_map/layer/pallas_call | solution.py:525
  69.0 2.4 %store.1 = (bf16[512,2048]{1,0:T(8,128)(2,1)}, bf16[512,2048]{1,0:T(8,128)(2,1)}, bf16[512,256]{1,0:T(8,128)(2,1)}, bf16[512,256]{1,0:T(8,128)(2,1)}, f32[64,512...) custom-call(bf16[512,2048]{1,0:T(8,128)(2,1)S(1)} %get-tuple-element.24.refs_0_, ...), custom_call_target="tpu_custom_call" | custom-call | tf_op jit(solution)/shard_map/store/pallas_call | solution.py:552

commit v4 on v3

--- a/solution.py
+++ b/solution.py
@@ -78,12 +78,12 @@
     def columns(g):
         return pl.ds(g * GROUP, GROUP)
 
+    def load_wide(d, g):
+        return load((x_hbm, go_hbm)[d].at[:, columns(g)], wide.at[d, :, columns(g)])
+
     small = [load(s, d) for s, d in ((dt_hbm, dt_v), (start_hbm, start_v), (al_hbm, al), (tb_hbm, tb), (sk_hbm, sk))]
-    narrow_in = [load(b_hbm, b_v), load(c_hbm, c_v)]
-    wide_in = [
-        [load(x_hbm.at[:, columns(g)], wide.at[0, :, columns(g)]), load(go_hbm.at[:, columns(g)], wide.at[1, :, columns(g)])]
-        for g in range(G)
-    ]
+    small += [load(b_hbm, b_v), load(c_hbm, c_v)]
+    wide_in = [[load_wide(0, 0), load_wide(1, 0)]]
 
     barrier = pltpu.get_barrier_semaphore()
 
@@ -104,25 +104,33 @@
         )
 
     def z_up(g):
-        return remote(part.at[1 - side, g], z_in.at[g], z_s_sem.at[g], z_r_sem.at[g], partner)
+        return remote(part.at[1 - side, g], z_in.at[g], z_s_sem.at[0], z_r_sem.at[g], partner)
 
     def z_decays():
-        return remote(ends_here, ends_there, z_s_sem.at[G], z_r_sem.at[G], partner)
+        return remote(ends_here, ends_there, z_s_sem.at[1], z_r_sem.at[G], partner)
 
     def up_rows(g):
         return pl.ds(8 + g * 2 * BAND, 2 * BAND) if g else pl.ds(0, 8 + 2 * BAND)
 
     def up_copy(g, k):
-        return remote(up.at[peer(k), up_rows(g)], up_in.at[place, up_rows(g)], up_s_sem.at[g, k], up_r_sem.at[g, k], near(k))
+        return remote(up.at[peer(k), up_rows(g)], up_in.at[place, up_rows(g)], up_s_sem.at[0], up_r_sem.at[g], near(k))
 
     def down_rows(g):
         return pl.ds(g * 2 * BAND, 2 * BAND)
 
     def down_copy(g, k):
-        return remote(down.at[peer(k), down_rows(g)], down_in.at[place, down_rows(g)], down_s_sem.at[g, k], down_r_sem.at[g, k], near(k))
+        return remote(down.at[peer(k), down_rows(g)], down_in.at[place, down_rows(g)], down_s_sem.at[0], down_r_sem.at[g], near(k))
 
     def z_back(g):
-        return remote(z_out.at[g], state.at[side, g], back_s_sem.at[g], back_r_sem.at[g], partner)
+        return remote(z_out.at[g], state.at[side, g], back_s_sem.at[0], back_r_sem.at[g], partner)
+
+    def received(ref, sem):
+        remote(ref, ref, z_s_sem.at[0], sem, partner).wait_recv()
+
+    def sent(ref, sem):
+        remote(ref, ref, sem, z_r_sem.at[0], partner).wait_send()
+
+    others = pl.ds(0, XY - 1)
 
     def each_peer(act):
         def body(k, carry):
@@ -144,8 +152,10 @@
     map_heads(0)
     lows = triangle(True)
     lows_half = lows.astype(BF16)
-    for copy in small + narrow_in:
+    for copy in small:
         copy.wait()
+    for g in range(1, G):
+        wide_in.append([load_wide(0, g), load_wide(1, g)])
     rate = -jnp.exp(al[...])
     lasts, spans = [], []
     for block in range(2):
@@ -366,7 +376,7 @@
         up_in[place, up_rows(g)] = up[place, up_rows(g)]
 
     def scan(g):
-        each_peer(lambda k: up_copy(g, k).wait_recv())
+        received(up_in.at[others, up_rows(g)], up_r_sem.at[g])
 
         def rise(j, now):
             down[j, pl.ds(2 * g * BAND, BAND)] = now
@@ -383,7 +393,7 @@
         down_in[place, down_rows(g)] = down[place, down_rows(g)]
 
     def spread(g):
-        each_peer(lambda k: down_copy(g, k).wait_recv())
+        received(down_in.at[others, down_rows(g)], down_r_sem.at[g])
         mine, theirs = factors()
         for s in range(2):
             at = pl.ds((2 * g + s) * BAND, BAND)
@@ -430,27 +440,25 @@
     final_sums(0)
     spread(G - 1)
     final_out(0)
-    for g in range(G):
-        z_up(g).wait_send()
-        each_peer(lambda k: up_copy(g, k).wait_send())
-        each_peer(lambda k: down_copy(g, k).wait_send())
     z_decays().wait_send()
+    sent(z_in, z_s_sem.at[0])
+    sent(up.at[others], up_s_sem.at[0])
+    sent(down.at[others], down_s_sem.at[0])
     weigh()
     for g in range(1, G - 1):
         z_back(g).wait_recv()
         final_sums(g)
         final_out(g)
     early_sums()
-    for g in range(G):
-        z_back(g).wait_send()
+    sent(z_out, back_s_sem.at[0])
     z_back(G - 1).wait_recv()
     params[...] = early_s[...] + last_sums()
 
     def sum1(k):
-        return remote(params, buf1.at[k], s1.at[k], r1.at[k], near(k))
+        return remote(params, buf1.at[k], s1.at[0], r1.at[0], near(k))
 
     def sum2(k):
-        return remote(buf2.at[0], buf2.at[k], s2.at[k], r2.at[k], far(k))
+        return remote(buf2.at[0], buf2.at[k], s2.at[0], r2.at[0], far(k))
 
     def each_far(act):
         def body(k, carry):
@@ -465,18 +473,18 @@
     final_out(G - 1)
     for block in range(2):
         gdt[:, block * STRETCH : (block + 1) * STRETCH] = jnp.transpose(dt_gradients(block)[1])
-    each_peer(lambda k: sum1(k).wait_recv())
+    received(buf1.at[pl.ds(1, XY - 1)], r1.at[0])
     buf2[0] = jnp.sum(buf1[...], axis=0)
     each_far(lambda k: sum2(k).start())
-    each_peer(lambda k: sum1(k).wait_send())
-    each_far(lambda k: sum2(k).wait_recv())
+    sent(buf1.at[pl.ds(1, XY - 1)], s1.at[0])
+    received(buf2.at[pl.ds(1, FAR - 1)], r2.at[0])
     total = jnp.zeros((8, H), F32)
     for g in range(FAR):
         total += buf2[lax.rem(g - mine_far + FAR, FAR)]
     grad_a[...] = total[0:1]
     grad_t[...] = total[1:2]
     grad_k[...] = total[2:3]
-    each_far(lambda k: sum2(k).wait_send())
+    sent(buf2.at[pl.ds(1, FAR - 1)], s2.at[0])
 
 
 def store_kernel(*refs):
@@ -539,9 +547,9 @@
             f32(2, G, 2, N, GROUP), f32(2, G, 2, N, GROUP), f32(G, 2, N, GROUP), f32(G, 2, N, GROUP),
             f32(XY, 8 + 2 * N, LANES), f32(XY, 8 + 2 * N, LANES), f32(XY, 2 * N, LANES), f32(XY, 2 * N, LANES),
             f32(8, H), f32(XY, 8, H), f32(FAR, 8, H),
-            dma((7 + 2 * G,)), dma((G + 1,)), dma((G + 1,)),
-            dma((G, XY)), dma((G, XY)), dma((G, XY)), dma((G, XY)), dma((G,)), dma((G,)),
-            dma((XY,)), dma((XY,)), dma((FAR,)), dma((FAR,)),
+            dma((7 + 2 * G,)), dma((2,)), dma((G + 1,)),
+            dma((1,)), dma((G,)), dma((1,)), dma((G,)), dma((1,)), dma((G,)),
+            dma((1,)), dma((1,)), dma((1,)), dma((1,)),
         ],
         compiler_params=pltpu.CompilerParams(
             collective_id=0, has_side_effects=True, vmem_limit_bytes=44 * 2**20

time: 71.7 us -> 68.2 us (0.951)
  Pallas kernels: 70.7 us -> 67.2 us
    pallas_call x1, Pallas kernels: 68.4 us -> 64.8 us  [shards(): pl.pallas_call(layer_kernel, out_shape=held, in_specs=[anywhere] * len(ar...]
where the time goes in v4:
time: 68.2 us; the launch traced here: 68 us
  Pallas kernels  67.2 us (99%)
  between operations  0.82 us (1%)
    pallas_call x1, Pallas kernels, shards(): pl.pallas_call(layer_kernel, out_shape=held, in_specs=[anywhere] * len(ar...  64.8 us
    pallas_call x1, Pallas kernels, shards(): pl.pallas_call(store_kernel, out_shape=outs, in_specs=[vmem] * len(outs),...  2.38 us

profile of v4, /device:TPU:1, one launch (start us, length us, event | category | flops | bytes accessed | tf_op | source)
XLA Modules:
  0.0 68.0 jit_solution(2500451250107595499)
XLA Ops:
  0.6 64.8 %layer.1 = (bf16[512,2048]{1,0:T(8,128)(2,1)S(1)}, bf16[512,2048]{1,0:T(8,128)(2,1)S(1)}, bf16[512,256]{1,0:T(8,128)(2,1)S(1)}, bf16[512,256]{1,0:T(8,128)(2,1)S...) custom-call(bf16[512,2048]{1,0:T(8,128)(2,1)} %bitcast.20, ...), custom_call_target="tpu_custom_call" | custom-call | flops 5000000000 | bytes 10485760 | tf_op jit(solution)/shard_map/layer/pallas_call | solution.py:533
  65.5 2.4 %store.1 = (bf16[512,2048]{1,0:T(8,128)(2,1)}, bf16[512,2048]{1,0:T(8,128)(2,1)}, bf16[512,256]{1,0:T(8,128)(2,1)}, bf16[512,256]{1,0:T(8,128)(2,1)}, f32[64,512...) custom-call(bf16[512,2048]{1,0:T(8,128)(2,1)S(1)} %get-tuple-element.24.refs_0_, ...), custom_call_target="tpu_custom_call" | custom-call | tf_op jit(solution)/shard_map/store/pallas_call | solution.py:560

commit v5 on v4

--- a/solution.py
+++ b/solution.py
@@ -455,10 +455,10 @@
     params[...] = early_s[...] + last_sums()
 
     def sum1(k):
-        return remote(params, buf1.at[k], s1.at[0], r1.at[0], near(k))
+        return remote(params, buf2.at[k], s2.at[0], r2.at[0], far(k))
 
     def sum2(k):
-        return remote(buf2.at[0], buf2.at[k], s2.at[0], r2.at[0], far(k))
+        return remote(buf1.at[0], buf1.at[k], s1.at[0], r1.at[0], near(k))
 
     def each_far(act):
         def body(k, carry):
@@ -467,24 +467,27 @@
 
         lax.fori_loop(1, FAR, body, 0)
 
-    each_peer(lambda k: sum1(k).start())
-    buf1[0] = params[...]
+    each_far(lambda k: sum1(k).start())
+    buf2[0] = params[...]
     final_sums(G - 1)
+    received(buf2.at[pl.ds(1, FAR - 1)], r2.at[0])
+    total = jnp.zeros((8, H), F32)
+    for g in range(FAR):
+        total += buf2[lax.rem(mine_far - g + FAR, FAR)]
+    buf1[0] = total
+    each_peer(lambda k: sum2(k).start())
     final_out(G - 1)
     for block in range(2):
         gdt[:, block * STRETCH : (block + 1) * STRETCH] = jnp.transpose(dt_gradients(block)[1])
+    sent(buf2.at[pl.ds(1, FAR - 1)], s2.at[0])
     received(buf1.at[pl.ds(1, XY - 1)], r1.at[0])
-    buf2[0] = jnp.sum(buf1[...], axis=0)
-    each_far(lambda k: sum2(k).start())
-    sent(buf1.at[pl.ds(1, XY - 1)], s1.at[0])
-    received(buf2.at[pl.ds(1, FAR - 1)], r2.at[0])
     total = jnp.zeros((8, H), F32)
-    for g in range(FAR):
-        total += buf2[lax.rem(g - mine_far + FAR, FAR)]
+    for g in range(XY):
+        total += buf1[lax.rem(place - g + XY, XY)]
     grad_a[...] = total[0:1]
     grad_t[...] = total[1:2]
     grad_k[...] = total[2:3]
-    sent(buf2.at[pl.ds(1, FAR - 1)], s2.at[0])
+    sent(buf1.at[pl.ds(1, XY - 1)], s1.at[0])
 
 
 def store_kernel(*refs):

time: 68.2 us -> 67.2 us (0.985)
  Pallas kernels: 67.2 us -> 66.3 us
    pallas_call x1, Pallas kernels: 64.8 us -> 63.9 us  [shards(): pl.pallas_call(layer_kernel, out_shape=held, in_specs=[anywhere] * len(ar...]
where the time goes in v5:
time: 67.2 us; the launch traced here: 67.1 us
  Pallas kernels  66.3 us (99%)
  between operations  0.8 us (1%)
    pallas_call x1, Pallas kernels, shards(): pl.pallas_call(layer_kernel, out_shape=held, in_specs=[anywhere] * len(ar...  63.9 us
    pallas_call x1, Pallas kernels, shards(): pl.pallas_call(store_kernel, out_shape=outs, in_specs=[vmem] * len(outs),...  2.38 us

profile of v5, /device:TPU:1, one launch (start us, length us, event | category | flops | bytes accessed | tf_op | source)
XLA Modules:
  0.0 67.1 jit_solution(16099135444879240202)
XLA Ops:
  0.6 63.9 %layer.1 = (bf16[512,2048]{1,0:T(8,128)(2,1)S(1)}, bf16[512,2048]{1,0:T(8,128)(2,1)S(1)}, bf16[512,256]{1,0:T(8,128)(2,1)S(1)}, bf16[512,256]{1,0:T(8,128)(2,1)S...) custom-call(bf16[512,2048]{1,0:T(8,128)(2,1)} %bitcast.20, ...), custom_call_target="tpu_custom_call" | custom-call | flops 5000000000 | bytes 10485760 | tf_op jit(solution)/shard_map/layer/pallas_call | solution.py:536
  64.5 2.4 %store.1 = (bf16[512,2048]{1,0:T(8,128)(2,1)}, bf16[512,2048]{1,0:T(8,128)(2,1)}, bf16[512,256]{1,0:T(8,128)(2,1)}, bf16[512,256]{1,0:T(8,128)(2,1)}, f32[64,512...) custom-call(bf16[512,2048]{1,0:T(8,128)(2,1)S(1)} %get-tuple-element.24.refs_0_, ...), custom_call_target="tpu_custom_call" | custom-call | tf_op jit(solution)/shard_map/store/pallas_call | solution.py:563

commit v6 on v5

--- a/solution.py
+++ b/solution.py
@@ -67,6 +67,19 @@
         g = lax.rem(mine_far + k, FAR)
         return {"dp": g // 2, "ctx": place * 2 + lax.rem(g, 2)}
 
+    barrier = pltpu.get_barrier_semaphore()
+
+    def greet_near(k, carry):
+        pl.semaphore_signal(barrier, inc=1, device_id=near(k), device_id_type=MESH)
+        return carry
+
+    def greet_far(k, carry):
+        pl.semaphore_signal(barrier, inc=1, device_id=far(k), device_id_type=MESH)
+        return carry
+
+    lax.fori_loop(1, FAR, greet_far, 0)
+    lax.fori_loop(1, XY, greet_near, 0)
+
     loads = []
 
     def load(src, dst):
@@ -84,19 +97,6 @@
     small = [load(s, d) for s, d in ((dt_hbm, dt_v), (start_hbm, start_v), (al_hbm, al), (tb_hbm, tb), (sk_hbm, sk))]
     small += [load(b_hbm, b_v), load(c_hbm, c_v)]
     wide_in = [[load_wide(0, 0), load_wide(1, 0)]]
-
-    barrier = pltpu.get_barrier_semaphore()
-
-    def greet_near(k, carry):
-        pl.semaphore_signal(barrier, inc=1, device_id=near(k), device_id_type=MESH)
-        return carry
-
-    def greet_far(k, carry):
-        pl.semaphore_signal(barrier, inc=1, device_id=far(k), device_id_type=MESH)
-        return carry
-
-    lax.fori_loop(1, XY, greet_near, 0)
-    lax.fori_loop(1, FAR, greet_far, 0)
 
     def remote(src, dst, send, recv, to):
         return pltpu.make_async_remote_copy(

time: 67.2 us -> 67.2 us (level)
  no operation moved by 1% of the time
where the time goes in v6:
time: 67.2 us; the launch traced here: 67.1 us
  Pallas kernels  66.3 us (99%)
  between operations  0.8 us (1%)
    pallas_call x1, Pallas kernels, shards(): pl.pallas_call(layer_kernel, out_shape=held, in_specs=[anywhere] * len(ar...  63.9 us
    pallas_call x1, Pallas kernels, shards(): pl.pallas_call(store_kernel, out_shape=outs, in_specs=[vmem] * len(outs),...  2.38 us

profile of v6, /device:TPU:1, one launch (start us, length us, event | category | flops | bytes accessed | tf_op | source)
XLA Modules:
  0.0 67.1 jit_solution(14165488024052534113)
XLA Ops:
  0.6 63.9 %layer.1 = (bf16[512,2048]{1,0:T(8,128)(2,1)S(1)}, bf16[512,2048]{1,0:T(8,128)(2,1)S(1)}, bf16[512,256]{1,0:T(8,128)(2,1)S(1)}, bf16[512,256]{1,0:T(8,128)(2,1)S...) custom-call(bf16[512,2048]{1,0:T(8,128)(2,1)} %bitcast.20, ...), custom_call_target="tpu_custom_call" | custom-call | flops 5000000000 | bytes 10485760 | tf_op jit(solution)/shard_map/layer/pallas_call | solution.py:536
  64.5 2.4 %store.1 = (bf16[512,2048]{1,0:T(8,128)(2,1)}, bf16[512,2048]{1,0:T(8,128)(2,1)}, bf16[512,256]{1,0:T(8,128)(2,1)}, bf16[512,256]{1,0:T(8,128)(2,1)}, f32[64,512...) custom-call(bf16[512,2048]{1,0:T(8,128)(2,1)S(1)} %get-tuple-element.24.refs_0_, ...), custom_call_target="tpu_custom_call" | custom-call | tf_op jit(solution)/shard_map/store/pallas_call | solution.py:563
